TPU v7x, 256 devices: a whole 4x4x8 slice. The times are simulated.
256 devices in a mesh: ctx: 16 (over y, x), head: 8 (over z_lo, core), pool: 2 (over z_hi).
Axes of the slice: x: 4, y: 4, z: 8 (z_hi: 2, z_lo: 4; z = z_hi * 4 + z_lo), core: 2. Of those that a mesh axis runs over, the one named last changes fastest.
Arguments:
- queries: bfloat16 [256, 64, 128], P(None, 'head'), may hold values from -200 to 200
- prefix_keys: bfloat16 [8192, 8, 128], P(('ctx', 'pool'), 'head'), may hold values from -6 to 6
- prefix_values: bfloat16 [8192, 8, 128], P(('ctx', 'pool'), 'head'), may hold values from -6 to 6
- new_states: bfloat16 [1536, 8192], P(None, ('ctx', 'pool')), may hold values from -7 to 7
- key_weight: bfloat16 [8192, 1024], P(('ctx', 'pool'), 'head'), may hold values from -0.0625 to 0.0625
- value_weight: bfloat16 [8192, 1024], P(('ctx', 'pool'), 'head'), may hold values from -0.0625 to 0.0625
- suffix_keys: bfloat16 [32, 256, 8, 128], P(('ctx', 'pool'), None, 'head'), may hold values from -8 to 8
- suffix_values: bfloat16 [32, 256, 8, 128], P(('ctx', 'pool'), None, 'head'), may hold values from -6 to 6
- suffix_lengths: int32 [32], P(('ctx', 'pool')), may hold values from 1 to 256
- assignment: int32 [256], replicated, may hold values from 0 to 31
- out_weight: bfloat16 [8192, 8192], P('head', ('ctx', 'pool')), may hold values from -0.25 to 0.25
Outputs:
- projected: bfloat16 [256, 8192], P('head', ('ctx', 'pool'))
- new_keys: bfloat16 [1536, 8, 128], P(('ctx', 'pool'), 'head')
- new_values: bfloat16 [1536, 8, 128], P(('ctx', 'pool'), 'head')
All inputs are finite; a program needn't handle non-finite values.
Results may differ from a plain program's by a relative error of at most 0.0102.
Values may be sent and summed in bfloat16 or wider, within the bound.
A program may use at most 64 MiB of HBM per device.

v0:
```python
import math

import jax
import jax.numpy as jnp
from jax import lax
from jax.sharding import PartitionSpec as P


def cut_along(x, dim, count):
    before, after = (x.shape[:dim], x.shape[dim + 1 :])
    return jnp.moveaxis(x.reshape(*before, count, -1, *after), dim, 0)


def sum_at_owner(x, axis, dim):
    count = lax.axis_size(axis)
    tiles = lax.all_to_all(cut_along(x, dim, count), axis, 0, 0, tiled=True)
    return jnp.sum(tiles, axis=0)


def copy_for_each(x, axis):
    count = lax.axis_size(axis)
    return lax.all_to_all(jnp.broadcast_to(x[None], (count, *x.shape)), axis, 0, 0, tiled=True)


def over_copies(x, axis):
    return copy_for_each(x, axis).max(axis=0)


def side_by_side(arrays, axis, dim, along):
    widths = [math.prod(a.shape[along:]) for a in arrays]
    both = jnp.concatenate(
        [a.reshape(*a.shape[:along], w) for a, w in zip(arrays, widths)], axis=along
    )
    result = sum_at_owner(both, axis, dim)
    tiles = jnp.split(result, [sum(widths[:k]) for k in range(1, len(widths))], axis=along)
    return tuple(
        (b.reshape(*result.shape[:along], *a.shape[along:]) for a, b in zip(arrays, tiles))
    )


def joined_along(tiles, dim):
    dims = list(tiles.shape[1:])
    dims[dim] *= tiles.shape[0]
    return jnp.moveaxis(tiles, 0, dim).reshape(dims)


def gathered_copies(x, axis, dim):
    tiles = copy_for_each(x, axis)
    return joined_along(tiles, dim)


def rotate(values, positions):
    half_dim = values.shape[-1] // 2
    frequency = jnp.exp(
        jnp.arange(half_dim, dtype=jnp.float32) * (-2.0 * math.log(500000.0) / values.shape[-1])
    )
    angles = positions.astype(jnp.float32)[:, None] * frequency[None, :]
    cosine = jnp.cos(angles)[:, None, :]
    sine_part = jnp.sin(angles)[:, None, :]
    front = values[..., :half_dim]
    second = values[..., half_dim:]
    return jnp.concatenate(
        [front * cosine - second * sine_part, second * cosine + front * sine_part], -1
    )


def partial_softmax(scores, values):
    maxima = jnp.max(scores, 1)
    weights = jnp.exp(scores - maxima[:, None])
    totals = jnp.sum(weights, 1)
    weighted = jnp.dot(weights.astype(jnp.bfloat16), values, preferred_element_type=jnp.float32)
    return (weighted, maxima, totals)


def combine_parts(former, latter):
    maxima = jnp.maximum(former[1], latter[1])
    scale_one = jnp.exp(former[1] - maxima)
    scale_two = jnp.exp(latter[1] - maxima)
    weighted = former[0] * scale_one[..., None] + latter[0] * scale_two[..., None]
    return (weighted, maxima, former[2] * scale_one + latter[2] * scale_two)


def body(
    queries,
    prefix_keys,
    prefix_values,
    new_states,
    key_weight,
    value_weight,
    suffix_keys,
    suffix_values,
    suffix_lengths,
    assignment,
    out_weight,
):
    shards = lax.axis_size(("ctx", "pool"))
    shard_index = lax.axis_index(("ctx", "pool"))
    kv_local = prefix_keys.shape[1]
    head_dim = prefix_keys.shape[2]
    kv_width = kv_local * head_dim
    new_dev = new_states.shape[0] // shards
    joined = jnp.concatenate([key_weight, value_weight], 1)
    summed = sum_at_owner(
        jnp.dot(new_states, joined, preferred_element_type=jnp.float32), ("ctx", "pool"), 0
    )
    proj_keys = summed[:, :kv_width]
    proj_values = summed[:, kv_width:]
    offset = prefix_keys.shape[0] * shards + shard_index * new_dev
    positions = offset + jnp.arange(new_dev, dtype=jnp.int32)
    new_keys = rotate(proj_keys.reshape(new_dev, kv_local, head_dim), positions).astype(
        jnp.bfloat16
    )
    new_values = proj_values.reshape(new_dev, kv_local, head_dim).astype(jnp.bfloat16)
    particles = queries.shape[0]
    group_size = queries.shape[1] // kv_local
    suffix_dev = suffix_keys.shape[0]
    suffix_len = suffix_keys.shape[1]
    suffix_ids = shard_index * suffix_dev + jnp.arange(suffix_dev, dtype=jnp.int32)
    usable = (assignment[:, None, None] == suffix_ids[None, :, None]) & (
        jnp.arange(suffix_len, dtype=jnp.int32)[None, None, :] < suffix_lengths[None, :, None]
    )
    side_count = suffix_dev * suffix_len
    usable = usable.reshape(particles, side_count)
    row_count = particles * group_size
    block_rows = math.gcd(row_count, 1024)
    block_count = row_count // block_rows
    usable_rows = jnp.broadcast_to(usable[:, None, :], (particles, group_size, side_count)).reshape(
        block_count, block_rows, side_count
    )
    inv_scale = head_dim ** (-0.5)
    cached_len = prefix_keys.shape[0]
    query_rows = queries.reshape(block_count, block_rows, head_dim)
    main_keys = jnp.concatenate(
        [prefix_keys[:, 0], suffix_keys[:, :, 0].reshape(side_count, head_dim)], 0
    )
    main_values = jnp.concatenate(
        [prefix_values[:, 0], suffix_values[:, :, 0].reshape(side_count, head_dim)], 0
    )

    def one_block(inputs, main_keys=main_keys, main_values=main_values):
        block_q, block_use = inputs
        scores = jnp.dot(block_q, main_keys.T, preferred_element_type=jnp.float32) * inv_scale
        scores = jnp.concatenate(
            [scores[:, :cached_len], jnp.where(block_use, scores[:, cached_len:], -jnp.inf)], 1
        )
        return partial_softmax(scores, main_values)

    weighted, maxima, totals = lax.map(one_block, (query_rows, usable_rows))
    flat_queries = query_rows.reshape(row_count, head_dim)
    newest = partial_softmax(
        jnp.dot(flat_queries, new_keys[:, 0].T, preferred_element_type=jnp.float32) * inv_scale,
        new_values[:, 0],
    )
    merged = combine_parts(
        (
            weighted.reshape(row_count, head_dim),
            maxima.reshape(row_count),
            totals.reshape(row_count),
        ),
        newest,
    )
    partials = [merged]
    weighted = jnp.stack(
        [item[0].reshape(particles, group_size, head_dim) for item in partials], 1
    ).reshape(particles, kv_local * group_size, head_dim)
    maxima = jnp.stack([item[1].reshape(particles, group_size) for item in partials], 1).reshape(
        particles, kv_local * group_size
    )
    totals = jnp.stack([item[2].reshape(particles, group_size) for item in partials], 1).reshape(
        particles, kv_local * group_size
    )
    maxima_all = over_copies(maxima, ("ctx", "pool"))
    factor = jnp.exp(maxima - maxima_all)
    summed_w, summed_t = side_by_side(
        (weighted * factor[..., None], totals * factor), ("ctx", "pool"), 0, 2
    )
    merged_share = (summed_w / summed_t[..., None]).astype(jnp.bfloat16)
    attention = gathered_copies(merged_share, ("ctx", "pool"), 0)
    flat_rows = attention.reshape(particles, kv_local * group_size * head_dim)
    projected = sum_at_owner(
        jnp.dot(flat_rows, out_weight, preferred_element_type=jnp.float32), "head", 0
    ).astype(jnp.bfloat16)
    return (projected, new_keys, new_values)


def solution(mesh):
    in_specs = (
        P(None, "head", None),
        P(("ctx", "pool"), "head", None),
        P(("ctx", "pool"), "head", None),
        P(None, ("ctx", "pool")),
        P(("ctx", "pool"), "head"),
        P(("ctx", "pool"), "head"),
        P(("ctx", "pool"), None, "head", None),
        P(("ctx", "pool"), None, "head", None),
        P(("ctx", "pool")),
        P(),
        P("head", ("ctx", "pool")),
    )
    out_specs = (
        P("head", ("ctx", "pool")),
        P(("ctx", "pool"), "head", None),
        P(("ctx", "pool"), "head", None),
    )
    return jax.shard_map(body, mesh=mesh, in_specs=in_specs, out_specs=out_specs, check_vma=False)
```

profile of v0, /device:TPU:1, one launch (start us, length us, event | category | flops | bytes accessed | tf_op | source)
XLA Modules:
  0.0 172.3 jit_solution(1097830348370516892)
XLA Ops:
  0.6 1.1 copy-done
  1.8 1.3 convolution_bitcast_fusion.1
  3.1 1.6 copy.39
  4.7 14.8 %all-to-all-start = ((f32[32,48,256]{2,1,0:T(8,128)}), f32[32,48,256]{2,1,0:T(8,128)}, u32[]{:S(2)}, u32[]{:S(2)}) async-start(f32[32,48,256]{2,1,0:T(8,128)} %bitcast.14), calls=%async_computation | async-start | bytes 3145728 | tf_op jit(solution)/shard_map/all_to_all | solution.py:16
  20.2 0.7 pad_maximum_fusion.1
  20.9 0.1 broadcast_and_fusion
  21.0 1.1 broadcast_in_dim.23
  22.1 12.7 %while.14 = (s32[]{:T(128)}, f32[2,1024,128]{2,1,0:T(8,128)}, f32[2,1024]{1,0:T(2,128)S(1)}, f32[2,1024]{1,0:T(2,128)S(1)}, bf16[2,1024,128]{2,1,0:T(8,128)(2,1)...) while((s32[]{:T(128)}, f32[2,1024,128]{2,1,0:T(8,128)}, ...), condition=%wide.region_4.5_spmd, body=%wide.region_0.4_spmd.sunk | while | flops 272889856 | bytes 34390348 | solution.py:148
  22.1 0.4 convolution_multiply_fusion.4
  22.5 0.6 copy-done.3
  23.1 0.4 copy.56
  23.6 0.3 fusion.57
  23.9 1.0 copy-done.1
  24.9 0.5 fusion.58
  25.5 1.0 copy-done.8
  26.5 1.9 %fusion.59 = f32[1024]{0:T(1024)S(1)} fusion(f32[1024,256]{0,1:T(8,128)} %copy-done.1, f32[1024,256]{0,1:T(8,128)} %copy-done.2, f32[1024]{0:T(1024)S(1)} %reduce_max.72), kind=kLoop, calls=%fused_computation.3.clone.1 | loop fusion | flops 1571840 | bytes 2105344 | tf_op jit(solution)/shard_map/while/body/eval_jaxpr/reduce_sum | solution.py:70
  28.4 0.4 convolution_multiply_fusion.4
  28.9 0.6 copy-done.3
  29.5 0.4 copy.56
  29.9 0.3 fusion.57
  30.2 1.0 copy-done.1
  31.3 0.5 fusion.58
  31.8 1.0 copy-done.8
  32.8 1.9 %fusion.59 = f32[1024]{0:T(1024)S(1)} fusion(f32[1024,256]{0,1:T(8,128)} %copy-done.1, f32[1024,256]{0,1:T(8,128)} %copy-done.2, f32[1024]{0:T(1024)S(1)} %reduce_max.72), kind=kLoop, calls=%fused_computation.3.clone.1 | loop fusion | flops 1571840 | bytes 2105344 | tf_op jit(solution)/shard_map/while/body/eval_jaxpr/reduce_sum | solution.py:70
  34.8 0.1 reshape.375
  34.9 0.1 reshape.377
  35.0 0.8 reshape.374
  35.8 0.7 copy.44
  36.5 0.1 reshape.376
  36.6 0.7 copy.45
  37.3 12.0 %all-to-all-done = f32[32,48,256]{2,1,0:T(8,128)} async-done(((f32[32,48,256]{2,1,0:T(8,128)}), f32[32,48,256]{2,1,0:T(8,128)}, u32[]{:S(2)}, u32[]{:S(2)}) %all-to-all-start) | async-done | bytes 1572896 | tf_op jit(solution)/shard_map/all_to_all | solution.py:16
  49.3 1.5 reduce_sum.47
  50.8 0.2 fusion.29
  51.0 0.4 copy-done.10
  51.4 0.3 fusion.41
  51.7 0.1 reduce_max.61
  51.9 0.7 broadcast_in_dim.24
  52.7 3.9 %all-to-all-start.1 = ((f32[32,256,8]{1,2,0:T(8,128)}), f32[32,256,8]{1,2,0:T(8,128)S(1)}, u32[]{:S(2)}, u32[]{:S(2)}) async-start(f32[32,256,8]{1,2,0:T(8,128)} %broadcast_in_dim.24), calls=%async_computation.1 | async-start | bytes 524288 | tf_op jit(solution)/shard_map/all_to_all | solution.py:22
  56.5 0.6 fusion.36
  57.1 1.6 bitcast_multiply_fusion
  58.7 0.1 reduce_max.64
  58.8 0.1 reduce_max.60
  59.0 0.1 reduce_sum.49
  59.1 0.7 copy.47
  59.9 0.1 copy.43
  60.0 1.5 fusion.9
  61.5 7.2 %all-to-all-done.1 = f32[32,256,8]{1,2,0:T(8,128)S(1)} async-done(((f32[32,256,8]{1,2,0:T(8,128)}), f32[32,256,8]{1,2,0:T(8,128)S(1)}, u32[]{:S(2)}, u32[]{:S(2)}) %all-to-all-start.1) | async-done | bytes 262176 | tf_op jit(solution)/shard_map/all_to_all | solution.py:22
  68.7 0.1 reduce_max.65
  68.9 0.1 copy.41
  69.0 0.1 copy.48
  69.1 0.8 exponential_multiply_fusion
  69.9 1.0 copy.49
  71.0 0.3 broadcast_multiply_fusion
  71.3 0.2 pad_maximum_fusion
  71.5 26.5 %all_to_all.25 = f32[32,8,8,129]{3,2,1,0:T(8,128)S(1)} all-to-all(f32[32,8,8,129]{3,2,1,0:T(8,128)S(1)} %pad_maximum_fusion), channel_id=1, replica_groups=mesh['ctx'=16,'head'=8,'pool'=2] {'ctx','pool'}, dimensions={0} | all-to-all | bytes 2113536 | tf_op jit(solution)/shard_map/all_to_all | solution.py:16
  98.0 0.1 reduce_sum.50
  98.4 0.1 broadcast_in_dim.25
  98.5 32.4 %all_to_all.26 = bf16[32,8,8,128]{3,1,2,0:T(8,128)(2,1)S(1)} all-to-all(bf16[32,8,8,128]{3,1,2,0:T(8,128)(2,1)S(1)} %broadcast_in_dim.25), channel_id=1, replica_groups=mesh['ctx'=16,'head'=8,'pool'=2] {'ctx','pool'}, dimensions={0} | all-to-all | bytes 1048576 | tf_op jit(solution)/shard_map/all_to_all | solution.py:22
  130.8 2.0 %fusion.10 = f32[8,32,256]{2,1,0:T(8,128)} fusion(bf16[8,32,1024]{2,1,0:T(8,128)(2,1)S(1)} %bitcast.72, bf16[1024,256]{1,0:T(8,128)(2,1)} %param.23), kind=kOutput, calls=%fused_computation.20 | convolution fusion | flops 134217728 | bytes 1310720 | tf_op jit(solution)/shard_map/dot_general | solution.py:181
  132.9 30.1 %all-to-all-start.4 = ((f32[8,32,256]{2,1,0:T(8,128)}), f32[8,32,256]{2,1,0:T(8,128)S(1)}, u32[]{:S(2)}, u32[]{:S(2)}) async-start(f32[8,32,256]{2,1,0:T(8,128)} %fusion.10), calls=%async_computation.4 | async-start | bytes 524288 | tf_op jit(solution)/shard_map/all_to_all | solution.py:16
  163.0 0.7 pad_maximum_fusion.3
  163.6 1.3 fusion.37
  165.0 6.7 %all-to-all-done.4 = f32[8,32,256]{2,1,0:T(8,128)S(1)} async-done(((f32[8,32,256]{2,1,0:T(8,128)}), f32[8,32,256]{2,1,0:T(8,128)S(1)}, u32[]{:S(2)}, u32[]{:S(2)}) %all-to-all-start.4) | async-done | bytes 262176 | tf_op jit(solution)/shard_map/all_to_all | solution.py:16
  171.7 0.6 reduce_sum.51
  (75 shorter events, 0.8 us)
Async XLA Ops:
  0.6 1.1 copy-start
  4.7 15.5 %copy-start.17 = (bf16[1,256,1,128]{3,1,2,0:T(8,128)(2,1)S(1)}, bf16[1,256,1,128]{3,1,2,0:T(8,128)(2,1)}, u32[]{:S(2)}) copy-start(bf16[1,256,1,128]{3,1,2,0:T(8,128)(2,1)} %param.19) | copy-start | bytes 196612
  4.7 15.5 %copy-start.18 = (bf16[256,1,128]{2,0,1:T(8,128)(2,1)S(1)}, bf16[256,1,128]{2,0,1:T(8,128)(2,1)}, u32[]{:S(2)}) copy-start(bf16[256,1,128]{2,0,1:T(8,128)(2,1)} %param.14) | copy-start | bytes 196612
  4.7 15.5 %copy-start.19 = (bf16[1,256,1,128]{3,1,2,0:T(8,128)(2,1)S(1)}, bf16[1,256,1,128]{3,1,2,0:T(8,128)(2,1)}, u32[]{:S(2)}) copy-start(bf16[1,256,1,128]{3,1,2,0:T(8,128)(2,1)} %param.20) | copy-start | bytes 196612
  4.7 15.5 %copy-start.20 = (bf16[256,1,128]{2,0,1:T(8,128)(2,1)S(1)}, bf16[256,1,128]{2,0,1:T(8,128)(2,1)}, u32[]{:S(2)}) copy-start(bf16[256,1,128]{2,0,1:T(8,128)(2,1)} %param.15) | copy-start | bytes 196612
  4.7 16.2 %copy-start.22 = (s32[256]{0:T(256)S(1)}, s32[256]{0:T(256)}, u32[]{:S(2)}) copy-start(s32[256]{0:T(256)} %param.22) | copy-start | bytes 3076
  4.7 17.3 %copy-start.4 = (bf16[256,8,128]{2,1,0:T(8,128)(2,1)S(1)}, bf16[256,8,128]{2,1,0:T(8,128)(2,1)}, u32[]{:S(2)}) copy-start(bf16[256,8,128]{2,1,0:T(8,128)(2,1)} %param.13) | copy-start | bytes 1572868
  4.7 44.5 %all-to-all-start = ((f32[32,48,256]{2,1,0:T(8,128)}), f32[32,48,256]{2,1,0:T(8,128)}, u32[]{:S(2)}, u32[]{:S(2)}) async-start(f32[32,48,256]{2,1,0:T(8,128)} %bitcast.14), calls=%async_computation | async-start | bytes 3145728 | tf_op jit(solution)/shard_map/all_to_all | solution.py:16
  22.1 1.0 copy-start.3
  23.5 1.3 copy-start.7
  23.6 1.3 copy-start.12
  23.8 1.0 copy-start.1
  23.9 1.6 copy-start.2
  24.9 3.5 %copy-start.5 = (bf16[256,8,128]{2,1,0:T(8,128)(2,1)S(1)}, bf16[256,8,128]{2,1,0:T(8,128)(2,1)}, u32[]{:S(2)}) copy-start(bf16[256,8,128]{2,1,0:T(8,128)(2,1)} %get-tuple-element.209) | copy-start | bytes 1572868 | tf_op jit(solution)/shard_map/while
  25.4 1.0 copy-start.8
  28.4 1.0 copy-start.3
  29.9 1.3 copy-start.7
  29.9 1.3 copy-start.12
  30.2 1.0 copy-start.1
  30.2 1.6 copy-start.2
  31.2 3.5 %copy-start.5 = (bf16[256,8,128]{2,1,0:T(8,128)(2,1)S(1)}, bf16[256,8,128]{2,1,0:T(8,128)(2,1)}, u32[]{:S(2)}) copy-start(bf16[256,8,128]{2,1,0:T(8,128)(2,1)} %get-tuple-element.209) | copy-start | bytes 1572868 | tf_op jit(solution)/shard_map/while
  31.8 1.0 copy-start.8
  50.8 0.6 copy-start.10
  51.0 7.8 %copy-start.13 = (bf16[48,1,64]{2,0,1:T(8,128)(2,1)}, bf16[48,1,64]{2,0,1:T(8,128)(2,1)S(1)}, u32[]{:S(2)}) copy-start(bf16[48,1,64]{2,0,1:T(8,128)(2,1)S(1)} %get-tuple-element.102) | copy-start | bytes 18436
  51.0 7.8 %copy-start.15 = (bf16[48,1,64]{2,0,1:T(8,128)(2,1)}, bf16[48,1,64]{2,0,1:T(8,128)(2,1)S(1)}, u32[]{:S(2)}) copy-start(bf16[48,1,64]{2,0,1:T(8,128)(2,1)S(1)} %get-tuple-element.103) | copy-start | bytes 18436
  51.7 7.3 %copy-start.6 = (f32[48,2048]{1,0:T(8,128)}, f32[48,2048]{1,0:T(8,128)S(1)}, u32[]{:S(2)}) copy-start(f32[48,2048]{1,0:T(8,128)S(1)} %get-tuple-element.107) | copy-start | bytes 1179652
  52.7 16.1 %all-to-all-start.1 = ((f32[32,256,8]{1,2,0:T(8,128)}), f32[32,256,8]{1,2,0:T(8,128)S(1)}, u32[]{:S(2)}, u32[]{:S(2)}) async-start(f32[32,256,8]{1,2,0:T(8,128)} %broadcast_in_dim.24), calls=%async_computation.1 | async-start | bytes 524288 | tf_op jit(solution)/shard_map/all_to_all | solution.py:22
  57.1 2.8 %copy-start.21 = (f32[2048]{0:T(1024)S(1)}, f32[2048]{0:T(1024)}, u32[]{:S(2)}) copy-start(f32[2048]{0:T(1024)} %get-tuple-element.104) | copy-start | bytes 24580
  59.9 9.2 %copy-start.11 = (f32[32,8,8,1]{0,2,3,1:T(8,128)S(1)}, f32[32,8,8,1]{0,2,3,1:T(8,128)}, u32[]{:S(2)}) copy-start(f32[32,8,8,1]{0,2,3,1:T(8,128)} %copy.47) | copy-start | bytes 24580
  60.0 11.0 %copy-start.9 = (f32[32,8,8]{2,1,0:T(8,128)S(1)}, f32[32,8,8]{2,1,0:T(8,128)}, u32[]{:S(2)}) copy-start(f32[32,8,8]{2,1,0:T(8,128)} %reshape.374) | copy-start | bytes 24580
  98.1 64.8 %copy-start.14 = (bf16[48,1,64]{2,0,1:T(8,128)(2,1)S(1)}, bf16[48,1,64]{2,0,1:T(8,128)(2,1)}, u32[]{:S(2)}) copy-start(bf16[48,1,64]{2,0,1:T(8,128)(2,1)} %copy-done.13) | copy-start | bytes 18436
  98.2 64.8 %copy-start.16 = (bf16[48,1,64]{2,0,1:T(8,128)(2,1)S(1)}, bf16[48,1,64]{2,0,1:T(8,128)(2,1)}, u32[]{:S(2)}) copy-start(bf16[48,1,64]{2,0,1:T(8,128)(2,1)} %copy-done.15) | copy-start | bytes 18436
  132.9 38.8 %all-to-all-start.4 = ((f32[8,32,256]{2,1,0:T(8,128)}), f32[8,32,256]{2,1,0:T(8,128)S(1)}, u32[]{:S(2)}, u32[]{:S(2)}) async-start(f32[8,32,256]{2,1,0:T(8,128)} %fusion.10), calls=%async_computation.4 | async-start | bytes 524288 | tf_op jit(solution)/shard_map/all_to_all | solution.py:16
where the time goes:
time: 173 us; the launch traced here: 172 us
  blocking collectives  58.9 us (34%)
  starting transfers between devices  48.7 us (28%)
  waiting for transfers between devices  25.8 us (15%)
  local copies, waits for them, and re-layouts  17.9 us (10%)
  other arithmetic  12 us (7%)
  matrix products  7.14 us (4%)
    all_to_all x2, starting transfers between devices, sum_at_owner(): tiles = lax.all_to_all(cut_along(x, dim, count), axis, 0, 0, tiled=True)  44.8 us
    all_to_all x1, blocking collectives, copy_for_each(): lax.all_to_all(jnp.broadcast_to(x[None], (count, *x.shape)), axis, 0, 0,...  32.4 us
    all_to_all x1, blocking collectives, sum_at_owner(): tiles = lax.all_to_all(cut_along(x, dim, count), axis, 0, 0, tiled=True)  26.5 us
    all_to_all x2, waiting for transfers between devices, sum_at_owner(): tiles = lax.all_to_all(cut_along(x, dim, count), axis, 0, 0, tiled=True)  18.6 us
    all_to_all x1, waiting for transfers between devices, copy_for_each(): lax.all_to_all(jnp.broadcast_to(x[None], (count, *x.shape)), axis, 0, 0,...  7.2 us
    while x28, local copies, waits for them, and re-layouts  5.23 us
    all_to_all x1, starting transfers between devices, copy_for_each(): lax.all_to_all(jnp.broadcast_to(x[None], (count, *x.shape)), axis, 0, 0,...  3.87 us
    reduce_sum x3, other arithmetic, partial_softmax(): totals = jnp.sum(weights, 1)  3.79 us
  transfers between devices with their start and end apart: 3, of which 3 were waited for; matrix products, arithmetic and copies ran while one was open for 11% of the time, Pallas kernels for 0%

commit v1 on v0

v1 whole, which is shorter than its diff:
```python
import functools
import math

import jax
import jax.numpy as jnp
import numpy as np
from jax import lax
from jax.experimental import pallas as pl
from jax.experimental.pallas import tpu as pltpu
from jax.sharding import PartitionSpec as P

F32 = jnp.float32
BF16 = jnp.bfloat16
NX = 4
PLANE = 16
POOL = 2
HEADS = 8
GROUP = 8
HD = 128
PREFIX = 8192
NEW = 1536
NEW_DEV = NEW // (PLANE * POOL)
NEW_CHIP = NEW_DEV * POOL
FEAT = 256
ROWS = 2048
CHUNK = 128
CACHED = 256
SUFFIX = 256
MSG = HD + 16
OUT_COLS = 256
SCALE = HD**-0.5


def rotary_tables():
    half = HD // 2
    frequency = np.exp(
        np.arange(half, dtype=np.float32) * np.float32(-2.0 * math.log(500000.0) / HD)
    ).astype(np.float32)
    positions = (PREFIX + np.arange(NEW)).astype(np.float32)
    angles = (positions[:, None] * frequency[None, :]).astype(np.float32).astype(np.float64)
    cosine = np.cos(angles).astype(np.float32)
    sine = np.sin(angles).astype(np.float32)
    both = np.concatenate([cosine, cosine, -sine, sine], 1)
    return both.reshape(PLANE * POOL, NEW_DEV, 2 * HD)


def mm(a, b, ca, cb):
    return lax.dot_general(a, b, (((ca,), (cb,)), ((), ())), preferred_element_type=F32)


def stat_rows(m, l):
    m1 = m.astype(BF16).astype(F32)
    r = m - m1
    m2 = r.astype(BF16).astype(F32)
    m3 = r - m2
    l1 = l.astype(BF16).astype(F32)
    r = l - l1
    l2 = r.astype(BF16).astype(F32)
    l3 = r - l2
    row = lax.broadcasted_iota(jnp.int32, (16, CHUNK), 0)
    out = jnp.zeros((16, CHUNK), F32)
    for k, part in enumerate((m1, m2, m3, l1, l2, l3)):
        out = jnp.where(row == k, jnp.broadcast_to(part, (16, CHUNK)), out)
    return out.astype(BF16)


def read_stats(tile):
    t = tile.astype(F32)
    m = (t[0:1] + t[1:2]) + t[2:3]
    l = (t[3:4] + t[4:5]) + t[5:6]
    return m, l


def kernel(
    q_hbm, pk_hbm, pv_hbm, st_hbm, kw_hbm, vw_hbm, sk_hbm, sv_hbm, len_ref, asg_ref, ow_hbm, rot_hbm,
    proj_ref, nk_ref, nv_ref,
    st_v, w_v, q_v, k_v, v_v, vt_v, ow_v, rot_v,
    kv_send, kv_recv, kvz_send, kvz_recv,
    acc_v, m_v, l_v,
    att_send, att_recv, attz_send, attz_recv,
    ag_v, part_v, out_send, out_recv,
    lsem, s1, r1, s2, r2, s3, r3, s4, r4, s5, r5, s6, r6,
):
    c = lax.axis_index("ctx")
    h = lax.axis_index("head")
    p = lax.axis_index("pool")
    y = c // NX
    x = c % NX

    def plane_peer(i):
        return ((y + i // NX) % NX) * NX + (x + i % NX) % NX

    def remote(src, dst, ss, rs, cc, hh, pp):
        return pltpu.make_async_remote_copy(
            src_ref=src, dst_ref=dst, send_sem=ss, recv_sem=rs,
            device_id={"ctx": cc, "head": hh, "pool": pp},
            device_id_type=pl.DeviceIdType.MESH,
        )

    barrier = pltpu.get_barrier_semaphore()

    def greet(i, carry):
        pl.semaphore_signal(
            barrier, inc=1, device_id={"ctx": plane_peer(i), "head": h, "pool": p},
            device_id_type=pl.DeviceIdType.MESH,
        )
        return carry

    lax.fori_loop(1, PLANE, greet, 0)
    pl.semaphore_signal(
        barrier, inc=1, device_id={"ctx": c, "head": h, "pool": 1 - p},
        device_id_type=pl.DeviceIdType.MESH,
    )

    def greet_head(j, carry):
        pl.semaphore_signal(
            barrier, inc=1, device_id={"ctx": c, "head": (h + j) % HEADS, "pool": p},
            device_id_type=pl.DeviceIdType.MESH,
        )
        return carry

    lax.fori_loop(1, HEADS, greet_head, 0)

    shard = c * POOL + p
    loads = [
        pltpu.make_async_copy(st_hbm, st_v, lsem.at[0]),
        pltpu.make_async_copy(kw_hbm, w_v.at[:, pl.ds(0, HD)], lsem.at[1]),
        pltpu.make_async_copy(vw_hbm, w_v.at[:, pl.ds(HD, HD)], lsem.at[2]),
        pltpu.make_async_copy(q_hbm, q_v, lsem.at[3]),
        pltpu.make_async_copy(pk_hbm, k_v.at[pl.ds(0, CACHED)], lsem.at[4]),
        pltpu.make_async_copy(sk_hbm, k_v.at[pl.ds(CACHED, SUFFIX)], lsem.at[5]),
        pltpu.make_async_copy(pv_hbm, v_v.at[pl.ds(0, CACHED)], lsem.at[6]),
        pltpu.make_async_copy(sv_hbm, v_v.at[pl.ds(CACHED, SUFFIX)], lsem.at[7]),
        pltpu.make_async_copy(rot_hbm.at[shard], rot_v, lsem.at[8]),
        pltpu.make_async_copy(ow_hbm, ow_v, lsem.at[9]),
    ]
    for copy in loads:
        copy.start()
    for copy in loads[:3]:
        copy.wait()
    pl.semaphore_wait(barrier, (PLANE - 1) + 1 + (HEADS - 1))

    for dy in (2, 1, 3, 0):
        yy = (y + dy) % NX
        first = pl.multiple_of(yy * (NX * NEW_CHIP), NX * NEW_CHIP)
        part = jnp.dot(st_v[pl.ds(first, NX * NEW_CHIP), :], w_v[...], preferred_element_type=F32)
        kv_send[pl.ds(yy * NX, NX)] = part.astype(BF16).reshape(NX, NEW_CHIP, 2 * HD)

        def send_kv(dx, carry, dy=dy, yy=yy):
            i = dy * NX + dx
            cc = yy * NX + (x + dx) % NX
            remote(kv_send.at[cc], kv_recv.at[i], s1.at[i], r1.at[i], cc, h, p).start()
            return carry

        lax.fori_loop(1 if dy == 0 else 0, NX, send_kv, 0)

    for copy in loads[3:8]:
        copy.wait()
    vt_v[...] = v_v[...].astype(F32).T.astype(BF16)
    suffix_id = shard
    lim = jnp.where(asg_ref[...] == suffix_id, len_ref[0], 0).astype(BF16)
    lim = jnp.broadcast_to(lim, (16, 256))

    def cached_block(b, carry):
        who = lax.broadcasted_iota(jnp.int32, (256, 256), 0)
        row = lax.broadcasted_iota(jnp.int32, (256, 256), 1)
        spread = jnp.where(who == b * 32 + row // GROUP, 1.0, 0.0).astype(BF16)
        lim_rows = mm(lim, spread, 1, 0)[0:1]
        qb = q_v[pl.ds(pl.multiple_of(b * 256, 256), 256), :]
        s = mm(k_v[...], qb, 1, 1) * SCALE
        key = lax.broadcasted_iota(jnp.int32, (SUFFIX, 256), 0).astype(F32)
        side = jnp.where(key < lim_rows, s[CACHED:], -jnp.inf)
        m = jnp.maximum(
            jnp.max(s[:CACHED], 0, keepdims=True), jnp.max(side, 0, keepdims=True)
        )
        main_e = jnp.exp(s[:CACHED] - m)
        side_e = jnp.exp(side - m)
        l = jnp.sum(main_e, 0, keepdims=True) + jnp.sum(side_e, 0, keepdims=True)
        e = jnp.concatenate([main_e.astype(BF16), side_e.astype(BF16)], 0)
        o = mm(vt_v[...], e, 1, 0)
        for k in range(2):
            lanes = slice(k * CHUNK, (k + 1) * CHUNK)
            acc_v[b * 2 + k] = o[:, lanes]
            m_v[b * 2 + k] = jnp.broadcast_to(m[:, lanes], (8, CHUNK))
            l_v[b * 2 + k] = jnp.broadcast_to(l[:, lanes], (8, CHUNK))
        return carry

    lax.fori_loop(0, 8, cached_block, 0)

    def sum_kv(i, acc):
        remote(kv_send.at[c], kv_recv.at[i], s1.at[i], r1.at[i], c, h, p).wait_recv()
        return acc + kv_recv[i].astype(F32)

    mine = jnp.dot(
        st_v[pl.ds(pl.multiple_of(c * NEW_CHIP, NEW_CHIP), NEW_CHIP), :], w_v[...],
        preferred_element_type=F32,
    )
    total = lax.fori_loop(1, PLANE, sum_kv, mine)
    low, high = total[:NEW_DEV], total[NEW_DEV:]
    first = p == 0
    kvz_send[...] = jnp.where(first, high, low).astype(BF16)
    swap = remote(kvz_send, kvz_recv, s2, r2, c, h, 1 - p)
    swap.start()
    kept = jnp.where(first, low, high)
    loads[8].wait()
    swap.wait_recv()
    kv = kept + kvz_recv[...].astype(F32)
    raw = kv[:, :HD]
    turned = pltpu.roll(raw, HD // 2, 1)
    new_k = (raw * rot_v[:, :HD] + turned * rot_v[:, HD:]).astype(BF16)
    new_v = kv[:, HD:].astype(BF16)
    nk_ref[...] = new_k
    nv_ref[...] = new_v
    new_vt = new_v.astype(F32).T.astype(BF16)

    def new_block(dy):
        yy = (y + dy) % NX
        qb = q_v[pl.ds(pl.multiple_of(yy * 512, 512), 512), :]
        s = mm(new_k, qb, 1, 1) * SCALE
        s_max = jnp.max(s, 0, keepdims=True)
        for k in range(NX):
            lanes = slice(k * CHUNK, (k + 1) * CHUNK)
            cc = yy * NX + k
            m_old = m_v[cc][0:1]
            m_new = jnp.maximum(m_old, s_max[:, lanes])
            shrink = jnp.exp(m_old - m_new)
            e = jnp.exp(s[:, lanes] - m_new)
            l_new = l_v[cc][0:1] * shrink + jnp.sum(e, 0, keepdims=True)
            o = acc_v[cc] * shrink + mm(new_vt, e.astype(BF16), 1, 0)
            att_send[cc, 0:HD] = o.astype(BF16)
            att_send[cc, HD:MSG] = stat_rows(m_new, l_new)
            if dy == 0:
                acc_v[cc] = o
                m_v[cc] = jnp.broadcast_to(m_new, (8, CHUNK))
                l_v[cc] = jnp.broadcast_to(l_new, (8, CHUNK))

    for dy in (2, 1, 3, 0):
        new_block(dy)

        def send_att(dx, carry, dy=dy):
            i = dy * NX + dx
            cc = ((y + dy) % NX) * NX + (x + dx) % NX
            remote(att_send.at[cc], att_recv.at[i], s3.at[i], r3.at[i], cc, h, p).start()
            return carry

        lax.fori_loop(1 if dy == 0 else 0, NX, send_att, 0)

    def merge(state, block):
        acc, m, l = state
        m_in, l_in = read_stats(block[HD:MSG])
        m_all = jnp.maximum(m, m_in)
        a = jnp.exp(m - m_all)
        b = jnp.exp(m_in - m_all)
        return (acc * a + block[0:HD].astype(F32) * b, m_all, l * a + l_in * b)

    def sum_att(i, state):
        remote(att_send.at[c], att_recv.at[i], s3.at[i], r3.at[i], c, h, p).wait_recv()
        return merge(state, att_recv[i])

    state = lax.fori_loop(1, PLANE, sum_att, (acc_v[c], m_v[c][0:1], l_v[c][0:1]))
    attz_send[0:HD] = state[0].astype(BF16)
    attz_send[HD:MSG] = stat_rows(state[1], state[2])
    swap_att = remote(attz_send, attz_recv, s4, r4, c, h, 1 - p)
    swap_att.start()
    swap_att.wait_recv()
    acc, _, l = merge(state, attz_recv[...])
    att = (acc / l).astype(BF16)
    to = lax.broadcasted_iota(jnp.int32, (CHUNK, CHUNK), 0)
    frm = lax.broadcasted_iota(jnp.int32, (CHUNK, CHUNK), 1)
    perm = jnp.where(frm == (to % 16) * GROUP + to // 16, 1.0, 0.0).astype(BF16)
    ag_v[c] = mm(perm, att, 1, 1).astype(BF16)

    def send_ag(i, carry):
        remote(ag_v.at[c], ag_v.at[c], s5.at[i], r5.at[i], plane_peer(i), h, p).start()
        return carry

    lax.fori_loop(1, PLANE, send_ag, 0)
    loads[9].wait()

    def wait_ag(i, carry):
        src = ((y + NX - i // NX) % NX) * NX + (x + NX - i % NX) % NX
        remote(ag_v.at[c], ag_v.at[src], s5.at[i], r5.at[i], c, h, p).wait_recv()
        return carry

    lax.fori_loop(1, PLANE, wait_ag, 0)

    out = jnp.zeros((256, OUT_COLS), F32)
    for g in range(GROUP):
        a = ag_v[:, g * 16:(g + 1) * 16, :].reshape(256, HD)
        out = out + jnp.dot(a, ow_v[g * HD:(g + 1) * HD, :], preferred_element_type=F32)
    part_v[...] = out.reshape(HEADS, 32, OUT_COLS)
    out_send[...] = out.astype(BF16).reshape(HEADS, 32, OUT_COLS)

    def send_out(j, carry):
        hh = (h + j) % HEADS
        remote(out_send.at[hh], out_recv.at[j], s6.at[j], r6.at[j], c, hh, p).start()
        return carry

    lax.fori_loop(1, HEADS, send_out, 0)

    def sum_out(j, acc):
        remote(out_send.at[h], out_recv.at[j], s6.at[j], r6.at[j], c, h, p).wait_recv()
        return acc + out_recv[j].astype(F32)

    proj_ref[...] = lax.fori_loop(1, HEADS, sum_out, part_v[h]).astype(BF16)

    def drain(i, carry):
        remote(kv_send.at[c], kv_recv.at[i], s1.at[i], r1.at[i], c, h, p).wait_send()
        remote(att_send.at[c], att_recv.at[i], s3.at[i], r3.at[i], c, h, p).wait_send()
        remote(ag_v.at[c], ag_v.at[c], s5.at[i], r5.at[i], c, h, p).wait_send()
        return carry

    lax.fori_loop(1, PLANE, drain, 0)
    swap.wait_send()
    swap_att.wait_send()

    def drain_out(j, carry):
        remote(out_send.at[h], out_recv.at[j], s6.at[j], r6.at[j], c, h, p).wait_send()
        return carry

    lax.fori_loop(1, HEADS, drain_out, 0)


def body(
    queries, prefix_keys, prefix_values, new_states, key_weight, value_weight,
    suffix_keys, suffix_values, suffix_lengths, assignment, out_weight,
):
    rot = jnp.asarray(rotary_tables())
    hbm = pl.BlockSpec(memory_space=pl.ANY)
    vmem = pl.BlockSpec(memory_space=pltpu.VMEM)
    smem = pl.BlockSpec(memory_space=pltpu.SMEM)
    dma = pltpu.SemaphoreType.DMA
    projected, new_keys, new_values = pl.pallas_call(
        kernel,
        out_shape=(
            jax.ShapeDtypeStruct((32, OUT_COLS), BF16),
            jax.ShapeDtypeStruct((NEW_DEV, HD), BF16),
            jax.ShapeDtypeStruct((NEW_DEV, HD), BF16),
        ),
        in_specs=[hbm] * 8 + [smem, vmem, hbm, hbm],
        out_specs=(vmem, vmem, vmem),
        scratch_shapes=[
            pltpu.VMEM((NEW, FEAT), BF16),
            pltpu.VMEM((FEAT, 2 * HD), BF16),
            pltpu.VMEM((ROWS, HD), BF16),
            pltpu.VMEM((CACHED + SUFFIX, HD), BF16),
            pltpu.VMEM((CACHED + SUFFIX, HD), BF16),
            pltpu.VMEM((HD, CACHED + SUFFIX), BF16),
            pltpu.VMEM((GROUP * HD, OUT_COLS), BF16),
            pltpu.VMEM((NEW_DEV, 2 * HD), F32),
            pltpu.VMEM((PLANE, NEW_CHIP, 2 * HD), BF16),
            pltpu.VMEM((PLANE, NEW_CHIP, 2 * HD), BF16),
            pltpu.VMEM((NEW_DEV, 2 * HD), BF16),
            pltpu.VMEM((NEW_DEV, 2 * HD), BF16),
            pltpu.VMEM((PLANE, HD, CHUNK), F32),
            pltpu.VMEM((PLANE, 8, CHUNK), F32),
            pltpu.VMEM((PLANE, 8, CHUNK), F32),
            pltpu.VMEM((PLANE, MSG, CHUNK), BF16),
            pltpu.VMEM((PLANE, MSG, CHUNK), BF16),
            pltpu.VMEM((MSG, CHUNK), BF16),
            pltpu.VMEM((MSG, CHUNK), BF16),
            pltpu.VMEM((PLANE, CHUNK, HD), BF16),
            pltpu.VMEM((HEADS, 32, OUT_COLS), F32),
            pltpu.VMEM((HEADS, 32, OUT_COLS), BF16),
            pltpu.VMEM((HEADS, 32, OUT_COLS), BF16),
            dma((10,)),
            dma((PLANE,)), dma((PLANE,)),
            dma, dma,
            dma((PLANE,)), dma((PLANE,)),
            dma, dma,
            dma((PLANE,)), dma((PLANE,)),
            dma((HEADS,)), dma((HEADS,)),
        ],
        compiler_params=pltpu.CompilerParams(
            collective_id=0, has_side_effects=True, vmem_limit_bytes=40 * 1024 * 1024
        ),
    )(
        queries.reshape(ROWS, HD),
        prefix_keys.reshape(CACHED, HD),
        prefix_values.reshape(CACHED, HD),
        new_states,
        key_weight,
        value_weight,
        suffix_keys.reshape(SUFFIX, HD),
        suffix_values.reshape(SUFFIX, HD),
        suffix_lengths,
        assignment.reshape(1, 256),
        out_weight,
        rot,
    )
    return (
        projected,
        new_keys.reshape(NEW_DEV, 1, HD),
        new_values.reshape(NEW_DEV, 1, HD),
    )


def solution(mesh):
    in_specs = (
        P(None, "head", None),
        P(("ctx", "pool"), "head", None),
        P(("ctx", "pool"), "head", None),
        P(None, ("ctx", "pool")),
        P(("ctx", "pool"), "head"),
        P(("ctx", "pool"), "head"),
        P(("ctx", "pool"), None, "head", None),
        P(("ctx", "pool"), None, "head", None),
        P(("ctx", "pool")),
        P(),
        P("head", ("ctx", "pool")),
    )
    out_specs = (
        P("head", ("ctx", "pool")),
        P(("ctx", "pool"), "head", None),
        P(("ctx", "pool"), "head", None),
    )
    return jax.shard_map(body, mesh=mesh, in_specs=in_specs, out_specs=out_specs, check_vma=False)
```

time: 173 us -> 67.1 us (0.39)
  blocking collectives: 58.9 us -> 0 us
  Pallas kernels: 0 us -> 53.1 us
  starting transfers between devices: 48.7 us -> 0 us
  waiting for transfers between devices: 25.8 us -> 0 us
  other arithmetic: 12 us -> 0 us
  matrix products: 7.14 us -> 0 us
  local copies, waits for them, and re-layouts: 17.9 us -> 12.1 us
    all_to_all x2 -> x0, blocking collectives: 58.8 us -> none  [the longest x1 32.4 us: copy_for_each(): lax.all_to_all(jnp.broadcast_to(x[None], (count, *x.shape)), axis, 0, 0,...]
    pallas_call x0 -> x1, Pallas kernels: none -> 53.1 us  [body(): pl.pallas_call(kernel, out_shape=(jax.ShapeDtypeStruct((32, OUT_COLS), BF...]
    all_to_all x3 -> x0, starting transfers between devices: 48.7 us -> none  [the longest x2 44.8 us: sum_at_owner(): tiles = lax.all_to_all(cut_along(x, dim, count), axis, 0, 0, tiled=True)]
    all_to_all x3 -> x0, waiting for transfers between devices: 25.8 us -> none  [the longest x2 18.6 us: sum_at_owner(): tiles = lax.all_to_all(cut_along(x, dim, count), axis, 0, 0, tiled=True)]
    unnamed x32 -> x25, local copies, waits for them, and re-layouts: 1.59 us -> 12.1 us
    dot_general x8 -> x0, matrix products: 7.14 us -> none  [the longest x3 2.61 us: partial_softmax(): jnp.dot(weights.astype(jnp.bfloat16), values, preferred_element_type=jnp....]
    reduce_sum x6 -> x0, other arithmetic: 6.07 us -> none  [the longest x3 3.79 us: partial_softmax(): totals = jnp.sum(weights, 1)]
    while x28 -> x0, local copies, waits for them, and re-layouts: 5.23 us -> none
  transfers between devices with their start and end apart: 3 -> 0, of which waited for: 3 -> 0; matrix products, arithmetic and copies ran while one was open for 11% -> 0% of each run, Pallas kernels for 0% -> 0%
where the time goes in v1:
time: 67.1 us; the launch traced here: 66.5 us
  Pallas kernels  53.1 us (79%)
  local copies, waits for them, and re-layouts  12.1 us (18%)
  between operations  1.31 us (2%)
    pallas_call x1, Pallas kernels, body(): pl.pallas_call(kernel, out_shape=(jax.ShapeDtypeStruct((32, OUT_COLS), BF...  53.1 us
    unnamed x25, local copies, waits for them, and re-layouts  12.1 us

profile of v1, /device:TPU:1, one launch (start us, length us, event | category | flops | bytes accessed | tf_op | source)
XLA Modules:
  0.0 66.5 jit_solution(14911362952534744135)
XLA Ops:
  1.3 0.0 copy-start
  1.3 1.4 %copy-done = f32[32,48,256]{2,1,0:T(8,128)S(1)} copy-done((f32[32,48,256]{2,1,0:T(8,128)S(1)}, f32[32,48,256]{2,1,0:T(8,128)}, u32[]{:S(2)}) %copy-start) | copy-done | bytes 1572888
  2.7 0.0 copy-start.1
  2.7 1.1 %copy-done.1 = bf16[1536,256]{1,0:T(8,128)(2,1)S(1)} copy-done((bf16[1536,256]{1,0:T(8,128)(2,1)S(1)}, bf16[1536,256]{1,0:T(8,128)(2,1)}, u32[]{:S(2)}) %copy-start.1) | copy-done | bytes 786456
  3.8 0.0 copy-start.2
  3.8 1.0 %copy-done.2 = bf16[256,8,128]{2,1,0:T(8,128)(2,1)S(1)} copy-done((bf16[256,8,128]{2,1,0:T(8,128)(2,1)S(1)}, bf16[256,8,128]{2,1,0:T(8,128)(2,1)}, u32[]{:S(2)}) %copy-start.2) | copy-done | bytes 524312
  4.9 0.0 copy-start.3
  4.9 1.0 %copy-done.3 = bf16[1024,256]{1,0:T(8,128)(2,1)S(1)} copy-done((bf16[1024,256]{1,0:T(8,128)(2,1)S(1)}, bf16[1024,256]{1,0:T(8,128)(2,1)}, u32[]{:S(2)}) %copy-start.3) | copy-done | bytes 524312
  5.9 0.0 copy-start.4
  5.9 0.8 %copy-done.4 = bf16[256,1,128]{2,0,1:T(8,128)(2,1)S(1)} copy-done((bf16[256,1,128]{2,0,1:T(8,128)(2,1)S(1)}, bf16[256,1,128]{2,0,1:T(8,128)(2,1)}, u32[]{:S(2)}) %copy-start.4) | copy-done | bytes 65560
  6.8 0.0 copy-start.5
  6.8 0.8 %copy-done.5 = bf16[256,1,128]{2,0,1:T(8,128)(2,1)S(1)} copy-done((bf16[256,1,128]{2,0,1:T(8,128)(2,1)S(1)}, bf16[256,1,128]{2,0,1:T(8,128)(2,1)}, u32[]{:S(2)}) %copy-start.5) | copy-done | bytes 65560
  7.6 0.0 copy-start.6
  7.6 0.8 %copy-done.6 = bf16[256,128]{1,0:T(8,128)(2,1)S(1)} copy-done((bf16[256,128]{1,0:T(8,128)(2,1)S(1)}, bf16[256,128]{1,0:T(8,128)(2,1)}, u32[]{:S(2)}) %copy-start.6) | copy-done | bytes 65560
  8.4 0.0 copy-start.7
  8.4 0.8 %copy-done.7 = bf16[256,128]{1,0:T(8,128)(2,1)S(1)} copy-done((bf16[256,128]{1,0:T(8,128)(2,1)S(1)}, bf16[256,128]{1,0:T(8,128)(2,1)}, u32[]{:S(2)}) %copy-start.7) | copy-done | bytes 65560
  9.3 0.0 copy-start.8
  9.3 0.8 %copy-done.8 = bf16[1,256,1,128]{3,1,2,0:T(8,128)(2,1)S(1)} copy-done((bf16[1,256,1,128]{3,1,2,0:T(8,128)(2,1)S(1)}, bf16[1,256,1,128]{3,1,2,0:T(8,128)(2,1)}, u32[]{:S(2)}) %copy-start.8) | copy-done | bytes 65560
  10.1 0.0 copy-start.9
  10.1 0.8 %copy-done.9 = bf16[1,256,1,128]{3,1,2,0:T(8,128)(2,1)S(1)} copy-done((bf16[1,256,1,128]{3,1,2,0:T(8,128)(2,1)S(1)}, bf16[1,256,1,128]{3,1,2,0:T(8,128)(2,1)}, u32[]{:S(2)}) %copy-start.9) | copy-done | bytes 65560
  10.9 0.0 copy-start.10
  11.0 0.7 %copy-done.10 = s32[256]{0:T(256)S(1)} copy-done((s32[256]{0:T(256)S(1)}, s32[256]{0:T(256)}, u32[]{:S(2)}) %copy-start.10) | copy-done | bytes 1048
  11.6 53.1 %shard_map.139 = (bf16[32,256]{1,0:T(8,128)(2,1)S(1)}, bf16[48,128]{1,0:T(8,128)(2,1)S(1)}, bf16[48,128]{1,0:T(8,128)(2,1)S(1)}) custom-call(bf16[2048,128]{1,0:T(8,128)(2,1)S(1)} %bitcast.8, bf16[256,128]{1,0:T(8,128)(2,1)S(1)} %bitcast.9, bf16[256,128]{1,0:T(8,128)(2,1)S(1)} %bitcast.10, bf16[1536,256]{1,0:T(8,128)(2,1)S(1)} %copy-done.1, ...), custom_call_target="tpu_custom_call" | custom-call | tf_op jit(solution)/shard_map/pallas_call | solution.py:333
  64.7 0.6 copy.19
  65.3 0.6 copy.20
  65.9 0.6 copy.21
Async XLA Ops:
  1.3 1.4 %copy-start = (f32[32,48,256]{2,1,0:T(8,128)S(1)}, f32[32,48,256]{2,1,0:T(8,128)}, u32[]{:S(2)}) copy-start(f32[32,48,256]{2,1,0:T(8,128)} %constant.2.clone.rot_hbm) | copy-start | bytes 4718596
  2.7 1.1 %copy-start.1 = (bf16[1536,256]{1,0:T(8,128)(2,1)S(1)}, bf16[1536,256]{1,0:T(8,128)(2,1)}, u32[]{:S(2)}) copy-start(bf16[1536,256]{1,0:T(8,128)(2,1)} %st_hbm.1) | copy-start | bytes 2359300
  3.8 1.0 %copy-start.2 = (bf16[256,8,128]{2,1,0:T(8,128)(2,1)S(1)}, bf16[256,8,128]{2,1,0:T(8,128)(2,1)}, u32[]{:S(2)}) copy-start(bf16[256,8,128]{2,1,0:T(8,128)(2,1)} %param.12) | copy-start | bytes 1572868
  4.9 1.0 %copy-start.3 = (bf16[1024,256]{1,0:T(8,128)(2,1)S(1)}, bf16[1024,256]{1,0:T(8,128)(2,1)}, u32[]{:S(2)}) copy-start(bf16[1024,256]{1,0:T(8,128)(2,1)} %ow_hbm.1) | copy-start | bytes 1572868
  5.9 0.8 %copy-start.4 = (bf16[256,1,128]{2,0,1:T(8,128)(2,1)S(1)}, bf16[256,1,128]{2,0,1:T(8,128)(2,1)}, u32[]{:S(2)}) copy-start(bf16[256,1,128]{2,0,1:T(8,128)(2,1)} %param.13) | copy-start | bytes 196612
  6.8 0.8 %copy-start.5 = (bf16[256,1,128]{2,0,1:T(8,128)(2,1)S(1)}, bf16[256,1,128]{2,0,1:T(8,128)(2,1)}, u32[]{:S(2)}) copy-start(bf16[256,1,128]{2,0,1:T(8,128)(2,1)} %param.14) | copy-start | bytes 196612
  7.6 0.8 %copy-start.6 = (bf16[256,128]{1,0:T(8,128)(2,1)S(1)}, bf16[256,128]{1,0:T(8,128)(2,1)}, u32[]{:S(2)}) copy-start(bf16[256,128]{1,0:T(8,128)(2,1)} %kw_hbm.1) | copy-start | bytes 196612
  8.4 0.8 %copy-start.7 = (bf16[256,128]{1,0:T(8,128)(2,1)S(1)}, bf16[256,128]{1,0:T(8,128)(2,1)}, u32[]{:S(2)}) copy-start(bf16[256,128]{1,0:T(8,128)(2,1)} %vw_hbm.1) | copy-start | bytes 196612
  9.3 0.8 %copy-start.8 = (bf16[1,256,1,128]{3,1,2,0:T(8,128)(2,1)S(1)}, bf16[1,256,1,128]{3,1,2,0:T(8,128)(2,1)}, u32[]{:S(2)}) copy-start(bf16[1,256,1,128]{3,1,2,0:T(8,128)(2,1)} %param.18) | copy-start | bytes 196612
  10.1 0.8 %copy-start.9 = (bf16[1,256,1,128]{3,1,2,0:T(8,128)(2,1)S(1)}, bf16[1,256,1,128]{3,1,2,0:T(8,128)(2,1)}, u32[]{:S(2)}) copy-start(bf16[1,256,1,128]{3,1,2,0:T(8,128)(2,1)} %param.19) | copy-start | bytes 196612
  10.9 0.7 %copy-start.10 = (s32[256]{0:T(256)S(1)}, s32[256]{0:T(256)}, u32[]{:S(2)}) copy-start(s32[256]{0:T(256)} %param.21) | copy-start | bytes 3076

commit v2 on v1

--- a/solution.py
+++ b/solution.py
@@ -72,9 +72,9 @@
 
 
 def kernel(
-    q_hbm, pk_hbm, pv_hbm, st_hbm, kw_hbm, vw_hbm, sk_hbm, sv_hbm, len_ref, asg_ref, ow_hbm, rot_hbm,
+    q_hbm, pk_hbm, pv_hbm, st_hbm, kw_hbm, vw_hbm, sk_hbm, sv_hbm, len_hbm, asg_hbm, ow_hbm, rot_hbm,
     proj_ref, nk_ref, nv_ref,
-    st_v, w_v, q_v, k_v, v_v, vt_v, ow_v, rot_v,
+    st_v, w_v, q_v, k_v, v_v, vt_v, ow_v, rot_v, len_v, asg_v,
     kv_send, kv_recv, kvz_send, kvz_recv,
     acc_v, m_v, l_v,
     att_send, att_recv, attz_send, attz_recv,
@@ -133,6 +133,8 @@
         pltpu.make_async_copy(sv_hbm, v_v.at[pl.ds(CACHED, SUFFIX)], lsem.at[7]),
         pltpu.make_async_copy(rot_hbm.at[shard], rot_v, lsem.at[8]),
         pltpu.make_async_copy(ow_hbm, ow_v, lsem.at[9]),
+        pltpu.make_async_copy(len_hbm, len_v, lsem.at[10]),
+        pltpu.make_async_copy(asg_hbm, asg_v, lsem.at[11]),
     ]
     for copy in loads:
         copy.start()
@@ -154,11 +156,11 @@
 
         lax.fori_loop(1 if dy == 0 else 0, NX, send_kv, 0)
 
-    for copy in loads[3:8]:
+    for copy in loads[3:8] + loads[10:]:
         copy.wait()
     vt_v[...] = v_v[...].astype(F32).T.astype(BF16)
     suffix_id = shard
-    lim = jnp.where(asg_ref[...] == suffix_id, len_ref[0], 0).astype(BF16)
+    lim = jnp.where(asg_v[...] == suffix_id, len_v[0], 0).astype(BF16)
     lim = jnp.broadcast_to(lim, (16, 256))
 
     def cached_block(b, carry):
@@ -328,7 +330,6 @@
     rot = jnp.asarray(rotary_tables())
     hbm = pl.BlockSpec(memory_space=pl.ANY)
     vmem = pl.BlockSpec(memory_space=pltpu.VMEM)
-    smem = pl.BlockSpec(memory_space=pltpu.SMEM)
     dma = pltpu.SemaphoreType.DMA
     projected, new_keys, new_values = pl.pallas_call(
         kernel,
@@ -337,7 +338,7 @@
             jax.ShapeDtypeStruct((NEW_DEV, HD), BF16),
             jax.ShapeDtypeStruct((NEW_DEV, HD), BF16),
         ),
-        in_specs=[hbm] * 8 + [smem, vmem, hbm, hbm],
+        in_specs=[hbm] * 12,
         out_specs=(vmem, vmem, vmem),
         scratch_shapes=[
             pltpu.VMEM((NEW, FEAT), BF16),
@@ -348,6 +349,8 @@
             pltpu.VMEM((HD, CACHED + SUFFIX), BF16),
             pltpu.VMEM((GROUP * HD, OUT_COLS), BF16),
             pltpu.VMEM((NEW_DEV, 2 * HD), F32),
+            pltpu.SMEM((1,), jnp.int32),
+            pltpu.VMEM((1, 256), jnp.int32),
             pltpu.VMEM((PLANE, NEW_CHIP, 2 * HD), BF16),
             pltpu.VMEM((PLANE, NEW_CHIP, 2 * HD), BF16),
             pltpu.VMEM((NEW_DEV, 2 * HD), BF16),
@@ -363,7 +366,7 @@
             pltpu.VMEM((HEADS, 32, OUT_COLS), F32),
             pltpu.VMEM((HEADS, 32, OUT_COLS), BF16),
             pltpu.VMEM((HEADS, 32, OUT_COLS), BF16),
-            dma((10,)),
+            dma((12,)),
             dma((PLANE,)), dma((PLANE,)),
             dma, dma,
             dma((PLANE,)), dma((PLANE,)),
@@ -372,7 +375,7 @@
             dma((HEADS,)), dma((HEADS,)),
         ],
         compiler_params=pltpu.CompilerParams(
-            collective_id=0, has_side_effects=True, vmem_limit_bytes=40 * 1024 * 1024
+            collective_id=0, has_side_effects=True, vmem_limit_bytes=60 * 1024 * 1024
         ),
     )(
         queries.reshape(ROWS, HD),

time: 67.1 us -> 59.8 us (0.89)
  local copies, waits for them, and re-layouts: 12.1 us -> 3.94 us
  Pallas kernels: 53.1 us -> 54.3 us
    unnamed x25 -> x3, local copies, waits for them, and re-layouts: 12.1 us -> 3.94 us
    pallas_call x1, Pallas kernels: 53.1 us -> 54.3 us  [body(): pl.pallas_call(kernel, out_shape=(jax.ShapeDtypeStruct((32, OUT_COLS), BF...]
where the time goes in v2:
time: 59.8 us; the launch traced here: 59.5 us
  Pallas kernels  54.3 us (91%)
  local copies, waits for them, and re-layouts  3.94 us (7%)
  between operations  1.29 us (2%)
    pallas_call x1, Pallas kernels, body(): pl.pallas_call(kernel, out_shape=(jax.ShapeDtypeStruct((32, OUT_COLS), BF...  54.3 us
    unnamed x3, local copies, waits for them, and re-layouts  3.94 us

profile of v2, /device:TPU:1, one launch (start us, length us, event | category | flops | bytes accessed | tf_op | source)
XLA Modules:
  0.0 59.5 jit_solution(576350223607457240)
XLA Ops:
  1.3 54.3 %shard_map.139 = (bf16[32,256]{1,0:T(8,128)(2,1)}, bf16[48,128]{1,0:T(8,128)(2,1)}, bf16[48,128]{1,0:T(8,128)(2,1)}) custom-call(bf16[2048,128]{1,0:T(8,128)(2,1)} %bitcast.8, bf16[256,128]{1,0:T(8,128)(2,1)} %bitcast.9, bf16[256,128]{1,0:T(8,128)(2,1)} %bitcast.10, bf16[1536,256]{1,0:T(8,128)(2,1)} %st_hbm.1, bf16[256,128]{1,0:T(8,128)(2,1)} %kw_hbm.1, ...), custom_call_target="tpu_custom_call" | custom-call | tf_op jit(solution)/shard_map/pallas_call | solution.py:334
  55.6 1.3 %copy.19 = bf16[32,256]{1,0:T(8,128)(2,1)} copy(bf16[32,256]{1,0:T(8,128)(2,1)} %get-tuple-element.12) | data formatting | bytes 32768
  56.9 1.3 %copy.20 = bf16[48,1,128]{2,0,1:T(8,128)(2,1)} copy(bf16[48,1,128]{2,0,1:T(8,128)(2,1)} %bitcast.14) | data formatting | bytes 24576
  58.2 1.3 %copy.21 = bf16[48,1,128]{2,0,1:T(8,128)(2,1)} copy(bf16[48,1,128]{2,0,1:T(8,128)(2,1)} %bitcast.13) | data formatting | bytes 24576

commit v3 on v2

--- a/solution.py
+++ b/solution.py
@@ -29,6 +29,7 @@
 MSG = HD + 16
 OUT_COLS = 256
 SCALE = HD**-0.5
+EARLY = 2
 
 
 def rotary_tables():
@@ -41,7 +42,7 @@
     cosine = np.cos(angles).astype(np.float32)
     sine = np.sin(angles).astype(np.float32)
     both = np.concatenate([cosine, cosine, -sine, sine], 1)
-    return both.reshape(PLANE * POOL, NEW_DEV, 2 * HD)
+    return both.reshape(PLANE, NEW_CHIP, 2 * HD)
 
 
 def mm(a, b, ca, cb):
@@ -75,11 +76,11 @@
     q_hbm, pk_hbm, pv_hbm, st_hbm, kw_hbm, vw_hbm, sk_hbm, sv_hbm, len_hbm, asg_hbm, ow_hbm, rot_hbm,
     proj_ref, nk_ref, nv_ref,
     st_v, w_v, q_v, k_v, v_v, vt_v, ow_v, rot_v, len_v, asg_v,
-    kv_send, kv_recv, kvz_send, kvz_recv,
+    key_send, key_recv, val_send, val_recv, keyz_send, keyz_recv, valz_send, valz_recv, valz_kept,
     acc_v, m_v, l_v,
     att_send, att_recv, attz_send, attz_recv,
     ag_v, part_v, out_send, out_recv,
-    lsem, s1, r1, s2, r2, s3, r3, s4, r4, s5, r5, s6, r6,
+    lsem, s1, r1, s2, r2, s3, r3, s4, r4, s5, r5, s6, r6, s7, r7, s8, r8,
 ):
     c = lax.axis_index("ctx")
     h = lax.axis_index("head")
@@ -96,30 +97,6 @@
             device_id={"ctx": cc, "head": hh, "pool": pp},
             device_id_type=pl.DeviceIdType.MESH,
         )
-
-    barrier = pltpu.get_barrier_semaphore()
-
-    def greet(i, carry):
-        pl.semaphore_signal(
-            barrier, inc=1, device_id={"ctx": plane_peer(i), "head": h, "pool": p},
-            device_id_type=pl.DeviceIdType.MESH,
-        )
-        return carry
-
-    lax.fori_loop(1, PLANE, greet, 0)
-    pl.semaphore_signal(
-        barrier, inc=1, device_id={"ctx": c, "head": h, "pool": 1 - p},
-        device_id_type=pl.DeviceIdType.MESH,
-    )
-
-    def greet_head(j, carry):
-        pl.semaphore_signal(
-            barrier, inc=1, device_id={"ctx": c, "head": (h + j) % HEADS, "pool": p},
-            device_id_type=pl.DeviceIdType.MESH,
-        )
-        return carry
-
-    lax.fori_loop(1, HEADS, greet_head, 0)
 
     shard = c * POOL + p
     loads = [
@@ -131,13 +108,38 @@
         pltpu.make_async_copy(sk_hbm, k_v.at[pl.ds(CACHED, SUFFIX)], lsem.at[5]),
         pltpu.make_async_copy(pv_hbm, v_v.at[pl.ds(0, CACHED)], lsem.at[6]),
         pltpu.make_async_copy(sv_hbm, v_v.at[pl.ds(CACHED, SUFFIX)], lsem.at[7]),
-        pltpu.make_async_copy(rot_hbm.at[shard], rot_v, lsem.at[8]),
+        pltpu.make_async_copy(rot_hbm.at[c], rot_v, lsem.at[8]),
         pltpu.make_async_copy(ow_hbm, ow_v, lsem.at[9]),
         pltpu.make_async_copy(len_hbm, len_v, lsem.at[10]),
         pltpu.make_async_copy(asg_hbm, asg_v, lsem.at[11]),
     ]
     for copy in loads:
         copy.start()
+
+    barrier = pltpu.get_barrier_semaphore()
+
+    def greet(i, carry):
+        pl.semaphore_signal(
+            barrier, inc=1, device_id={"ctx": plane_peer(i), "head": h, "pool": p},
+            device_id_type=pl.DeviceIdType.MESH,
+        )
+        return carry
+
+    lax.fori_loop(1, PLANE, greet, 0)
+    pl.semaphore_signal(
+        barrier, inc=1, device_id={"ctx": c, "head": h, "pool": 1 - p},
+        device_id_type=pl.DeviceIdType.MESH,
+    )
+
+    def greet_head(j, carry):
+        pl.semaphore_signal(
+            barrier, inc=1, device_id={"ctx": c, "head": (h + j) % HEADS, "pool": p},
+            device_id_type=pl.DeviceIdType.MESH,
+        )
+        return carry
+
+    lax.fori_loop(1, HEADS, greet_head, 0)
+
     for copy in loads[:3]:
         copy.wait()
     pl.semaphore_wait(barrier, (PLANE - 1) + 1 + (HEADS - 1))
@@ -146,15 +148,22 @@
         yy = (y + dy) % NX
         first = pl.multiple_of(yy * (NX * NEW_CHIP), NX * NEW_CHIP)
         part = jnp.dot(st_v[pl.ds(first, NX * NEW_CHIP), :], w_v[...], preferred_element_type=F32)
-        kv_send[pl.ds(yy * NX, NX)] = part.astype(BF16).reshape(NX, NEW_CHIP, 2 * HD)
-
-        def send_kv(dx, carry, dy=dy, yy=yy):
+        part = part.astype(BF16)
+        key_send[pl.ds(yy * NX, NX)] = part[:, :HD].reshape(NX, NEW_CHIP, HD)
+        val_send[pl.ds(yy * NX, NX)] = part[:, HD:].reshape(NX, NEW_CHIP, HD)
+
+        def send_keys(dx, carry, dy=dy, yy=yy):
             i = dy * NX + dx
             cc = yy * NX + (x + dx) % NX
-            remote(kv_send.at[cc], kv_recv.at[i], s1.at[i], r1.at[i], cc, h, p).start()
+            remote(key_send.at[cc], key_recv.at[i], s1.at[i], r1.at[i], cc, h, p).start()
             return carry
 
-        lax.fori_loop(1 if dy == 0 else 0, NX, send_kv, 0)
+        lax.fori_loop(1 if dy == 0 else 0, NX, send_keys, 0)
+
+    def send_values(i, carry):
+        cc = plane_peer(i)
+        remote(val_send.at[cc], val_recv.at[i], s7.at[i], r7.at[i], cc, h, p).start()
+        return carry
 
     for copy in loads[3:8] + loads[10:]:
         copy.wait()
@@ -187,33 +196,42 @@
             l_v[b * 2 + k] = jnp.broadcast_to(l[:, lanes], (8, CHUNK))
         return carry
 
-    lax.fori_loop(0, 8, cached_block, 0)
-
-    def sum_kv(i, acc):
-        remote(kv_send.at[c], kv_recv.at[i], s1.at[i], r1.at[i], c, h, p).wait_recv()
-        return acc + kv_recv[i].astype(F32)
+    lax.fori_loop(0, EARLY, cached_block, 0)
+    lax.fori_loop(1, PLANE, send_values, 0)
+    lax.fori_loop(EARLY, 8, cached_block, 0)
 
     mine = jnp.dot(
         st_v[pl.ds(pl.multiple_of(c * NEW_CHIP, NEW_CHIP), NEW_CHIP), :], w_v[...],
         preferred_element_type=F32,
     )
-    total = lax.fori_loop(1, PLANE, sum_kv, mine)
-    low, high = total[:NEW_DEV], total[NEW_DEV:]
+
+    def sum_keys(i, acc):
+        remote(key_send.at[c], key_recv.at[i], s1.at[i], r1.at[i], c, h, p).wait_recv()
+        return acc + key_recv[i].astype(F32)
+
+    keyz_send[...] = lax.fori_loop(1, PLANE, sum_keys, mine[:, :HD])
+    swap = remote(keyz_send, keyz_recv, s2, r2, c, h, 1 - p)
+    swap.start()
+
+    def sum_values(i, acc):
+        remote(val_send.at[c], val_recv.at[i], s7.at[i], r7.at[i], c, h, p).wait_recv()
+        return acc + val_recv[i].astype(F32)
+
+    values = lax.fori_loop(1, PLANE, sum_values, mine[:, HD:])
     first = p == 0
-    kvz_send[...] = jnp.where(first, high, low).astype(BF16)
-    swap = remote(kvz_send, kvz_recv, s2, r2, c, h, 1 - p)
-    swap.start()
-    kept = jnp.where(first, low, high)
+    valz_send[...] = jnp.where(first, values[NEW_DEV:], values[:NEW_DEV]).astype(BF16)
+    valz_kept[...] = jnp.where(first, values[:NEW_DEV], values[NEW_DEV:])
+    swap_values = remote(valz_send, valz_recv, s8, r8, c, h, 1 - p)
+    swap_values.start()
+    new_vt = values.T.astype(BF16)
     loads[8].wait()
     swap.wait_recv()
-    kv = kept + kvz_recv[...].astype(F32)
-    raw = kv[:, :HD]
+    raw = keyz_send[...] + keyz_recv[...]
     turned = pltpu.roll(raw, HD // 2, 1)
     new_k = (raw * rot_v[:, :HD] + turned * rot_v[:, HD:]).astype(BF16)
-    new_v = kv[:, HD:].astype(BF16)
-    nk_ref[...] = new_k
-    nv_ref[...] = new_v
-    new_vt = new_v.astype(F32).T.astype(BF16)
+    nk_ref[...] = jnp.where(first, new_k[:NEW_DEV], new_k[NEW_DEV:])
+    token = lax.broadcasted_iota(jnp.int32, (NEW_CHIP, CHUNK), 0)
+    counted = jnp.where((token // NEW_DEV) == p, 1.0, 0.0).astype(F32)
 
     def new_block(dy):
         yy = (y + dy) % NX
@@ -227,7 +245,7 @@
             m_new = jnp.maximum(m_old, s_max[:, lanes])
             shrink = jnp.exp(m_old - m_new)
             e = jnp.exp(s[:, lanes] - m_new)
-            l_new = l_v[cc][0:1] * shrink + jnp.sum(e, 0, keepdims=True)
+            l_new = l_v[cc][0:1] * shrink + jnp.sum(e * counted, 0, keepdims=True)
             o = acc_v[cc] * shrink + mm(new_vt, e.astype(BF16), 1, 0)
             att_send[cc, 0:HD] = o.astype(BF16)
             att_send[cc, HD:MSG] = stat_rows(m_new, l_new)
@@ -304,16 +322,21 @@
         remote(out_send.at[h], out_recv.at[j], s6.at[j], r6.at[j], c, h, p).wait_recv()
         return acc + out_recv[j].astype(F32)
 
+    swap_values.wait_recv()
+    nv_ref[...] = (valz_kept[...] + valz_recv[...].astype(F32)).astype(BF16)
+
     proj_ref[...] = lax.fori_loop(1, HEADS, sum_out, part_v[h]).astype(BF16)
 
     def drain(i, carry):
-        remote(kv_send.at[c], kv_recv.at[i], s1.at[i], r1.at[i], c, h, p).wait_send()
+        remote(key_send.at[c], key_recv.at[i], s1.at[i], r1.at[i], c, h, p).wait_send()
+        remote(val_send.at[c], val_recv.at[i], s7.at[i], r7.at[i], c, h, p).wait_send()
         remote(att_send.at[c], att_recv.at[i], s3.at[i], r3.at[i], c, h, p).wait_send()
         remote(ag_v.at[c], ag_v.at[c], s5.at[i], r5.at[i], c, h, p).wait_send()
         return carry
 
     lax.fori_loop(1, PLANE, drain, 0)
     swap.wait_send()
+    swap_values.wait_send()
     swap_att.wait_send()
 
     def drain_out(j, carry):
@@ -348,13 +371,18 @@
             pltpu.VMEM((CACHED + SUFFIX, HD), BF16),
             pltpu.VMEM((HD, CACHED + SUFFIX), BF16),
             pltpu.VMEM((GROUP * HD, OUT_COLS), BF16),
-            pltpu.VMEM((NEW_DEV, 2 * HD), F32),
+            pltpu.VMEM((NEW_CHIP, 2 * HD), F32),
             pltpu.SMEM((1,), jnp.int32),
             pltpu.VMEM((1, 256), jnp.int32),
-            pltpu.VMEM((PLANE, NEW_CHIP, 2 * HD), BF16),
-            pltpu.VMEM((PLANE, NEW_CHIP, 2 * HD), BF16),
-            pltpu.VMEM((NEW_DEV, 2 * HD), BF16),
-            pltpu.VMEM((NEW_DEV, 2 * HD), BF16),
+            pltpu.VMEM((PLANE, NEW_CHIP, HD), BF16),
+            pltpu.VMEM((PLANE, NEW_CHIP, HD), BF16),
+            pltpu.VMEM((PLANE, NEW_CHIP, HD), BF16),
+            pltpu.VMEM((PLANE, NEW_CHIP, HD), BF16),
+            pltpu.VMEM((NEW_CHIP, HD), F32),
+            pltpu.VMEM((NEW_CHIP, HD), F32),
+            pltpu.VMEM((NEW_DEV, HD), BF16),
+            pltpu.VMEM((NEW_DEV, HD), BF16),
+            pltpu.VMEM((NEW_DEV, HD), F32),
             pltpu.VMEM((PLANE, HD, CHUNK), F32),
             pltpu.VMEM((PLANE, 8, CHUNK), F32),
             pltpu.VMEM((PLANE, 8, CHUNK), F32),
@@ -373,9 +401,11 @@
             dma, dma,
             dma((PLANE,)), dma((PLANE,)),
             dma((HEADS,)), dma((HEADS,)),
+            dma((PLANE,)), dma((PLANE,)),
+            dma, dma,
         ],
         compiler_params=pltpu.CompilerParams(
-            collective_id=0, has_side_effects=True, vmem_limit_bytes=60 * 1024 * 1024
+            collective_id=0, has_side_effects=True, vmem_limit_bytes=55168 * 1024
         ),
     )(
         queries.reshape(ROWS, HD),

time: 59.8 us -> 54.3 us (0.908)
  Pallas kernels: 54.3 us -> 50.4 us
  local copies, waits for them, and re-layouts: 3.94 us -> 2.48 us
    pallas_call x1, Pallas kernels: 54.3 us -> 50.4 us  [body(): pl.pallas_call(kernel, out_shape=(jax.ShapeDtypeStruct((32, OUT_COLS), BF...]
    unnamed x3 -> x5, local copies, waits for them, and re-layouts: 3.94 us -> 2.48 us
where the time goes in v3:
time: 54.3 us; the launch traced here: 54.1 us
  Pallas kernels  50.4 us (93%)
  local copies, waits for them, and re-layouts  2.48 us (5%)
  between operations  1.3 us (2%)
    pallas_call x1, Pallas kernels, body(): pl.pallas_call(kernel, out_shape=(jax.ShapeDtypeStruct((32, OUT_COLS), BF...  50.4 us
    unnamed x5, local copies, waits for them, and re-layouts  2.48 us

profile of v3, /device:TPU:1, one launch (start us, length us, event | category | flops | bytes accessed | tf_op | source)
XLA Modules:
  0.0 54.1 jit_solution(6280527061328072702)
XLA Ops:
  1.3 0.0 copy-start
  1.3 0.7 %copy-done = s32[256]{0:T(256)S(1)} copy-done((s32[256]{0:T(256)S(1)}, s32[256]{0:T(256)}, u32[]{:S(2)}) %copy-start) | copy-done | bytes 1048
  2.0 50.4 %shard_map.139 = (bf16[32,256]{1,0:T(8,128)(2,1)S(1)}, bf16[48,128]{1,0:T(8,128)(2,1)S(1)}, bf16[48,128]{1,0:T(8,128)(2,1)S(1)}) custom-call(bf16[2048,128]{1,0:T(8,128)(2,1)} %bitcast.11, bf16[256,128]{1,0:T(8,128)(2,1)} %bitcast.12, bf16[256,128]{1,0:T(8,128)(2,1)} %bitcast.13, bf16[1536,256]{1,0:T(8,128)(2,1)} %st_hbm.1, bf16[256,128]{1,0:T(8,128)(2,1)} %kw_hbm.1, ...), custom_call_target="tpu_custom_call" | custom-call | tf_op jit(solution)/shard_map/pallas_call | solution.py:357
  52.3 0.6 %copy.19 = bf16[32,256]{1,0:T(8,128)(2,1)} copy(bf16[32,256]{1,0:T(8,128)(2,1)S(1)} %get-tuple-element.12) | data formatting | bytes 32768
  52.9 0.6 %copy.20 = bf16[48,1,128]{2,0,1:T(8,128)(2,1)} copy(bf16[48,1,128]{2,0,1:T(8,128)(2,1)S(1)} %bitcast.9) | data formatting | bytes 24576
  53.5 0.6 %copy.21 = bf16[48,1,128]{2,0,1:T(8,128)(2,1)} copy(bf16[48,1,128]{2,0,1:T(8,128)(2,1)S(1)} %bitcast.8) | data formatting | bytes 24576
Async XLA Ops:
  1.3 0.7 %copy-start = (s32[256]{0:T(256)S(1)}, s32[256]{0:T(256)}, u32[]{:S(2)}) copy-start(s32[256]{0:T(256)} %param.21) | copy-start | bytes 3076

commit v4 on v3

--- a/solution.py
+++ b/solution.py
@@ -29,7 +29,13 @@
 MSG = HD + 16
 OUT_COLS = 256
 SCALE = HD**-0.5
-EARLY = 2
+
+
+def hops(i):
+    return sum(min(d, NX - d) for d in (i % NX, i // NX))
+
+
+FARTHEST = sorted(range(1, PLANE), key=lambda i: -hops(i))
 
 
 def rotary_tables():
@@ -97,6 +103,20 @@
             device_id={"ctx": cc, "head": hh, "pool": pp},
             device_id_type=pl.DeviceIdType.MESH,
         )
+
+    barrier = pltpu.get_barrier_semaphore()
+
+    def greet(cc, hh, pp):
+        pl.semaphore_signal(
+            barrier, inc=1, device_id={"ctx": cc, "head": hh, "pool": pp},
+            device_id_type=pl.DeviceIdType.MESH,
+        )
+
+    for i in FARTHEST:
+        greet(plane_peer(i), h, p)
+    greet(c, h, 1 - p)
+    for j in range(1, HEADS):
+        greet(c, (h + j) % HEADS, p)
 
     shard = c * POOL + p
     loads = [
@@ -116,54 +136,28 @@
     for copy in loads:
         copy.start()
 
-    barrier = pltpu.get_barrier_semaphore()
-
-    def greet(i, carry):
-        pl.semaphore_signal(
-            barrier, inc=1, device_id={"ctx": plane_peer(i), "head": h, "pool": p},
-            device_id_type=pl.DeviceIdType.MESH,
-        )
-        return carry
-
-    lax.fori_loop(1, PLANE, greet, 0)
-    pl.semaphore_signal(
-        barrier, inc=1, device_id={"ctx": c, "head": h, "pool": 1 - p},
-        device_id_type=pl.DeviceIdType.MESH,
-    )
-
-    def greet_head(j, carry):
-        pl.semaphore_signal(
-            barrier, inc=1, device_id={"ctx": c, "head": (h + j) % HEADS, "pool": p},
-            device_id_type=pl.DeviceIdType.MESH,
-        )
-        return carry
-
-    lax.fori_loop(1, HEADS, greet_head, 0)
-
     for copy in loads[:3]:
         copy.wait()
+
+    for k in range(NX):
+        rows = pl.ds(k * NX * NEW_CHIP, NX * NEW_CHIP)
+        part = jnp.dot(st_v[rows, :], w_v[...], preferred_element_type=F32).astype(BF16)
+        key_send[k * NX:(k + 1) * NX] = part[:, :HD].reshape(NX, NEW_CHIP, HD)
+        val_send[k * NX:(k + 1) * NX] = part[:, HD:].reshape(NX, NEW_CHIP, HD)
     pl.semaphore_wait(barrier, (PLANE - 1) + 1 + (HEADS - 1))
-
-    for dy in (2, 1, 3, 0):
-        yy = (y + dy) % NX
-        first = pl.multiple_of(yy * (NX * NEW_CHIP), NX * NEW_CHIP)
-        part = jnp.dot(st_v[pl.ds(first, NX * NEW_CHIP), :], w_v[...], preferred_element_type=F32)
-        part = part.astype(BF16)
-        key_send[pl.ds(yy * NX, NX)] = part[:, :HD].reshape(NX, NEW_CHIP, HD)
-        val_send[pl.ds(yy * NX, NX)] = part[:, HD:].reshape(NX, NEW_CHIP, HD)
-
-        def send_keys(dx, carry, dy=dy, yy=yy):
-            i = dy * NX + dx
-            cc = yy * NX + (x + dx) % NX
-            remote(key_send.at[cc], key_recv.at[i], s1.at[i], r1.at[i], cc, h, p).start()
-            return carry
-
-        lax.fori_loop(1 if dy == 0 else 0, NX, send_keys, 0)
-
-    def send_values(i, carry):
+    for i in FARTHEST:
+        cc = plane_peer(i)
+        remote(key_send.at[cc], key_recv.at[i], s1.at[i], r1.at[i], cc, h, p).start()
+    for i in FARTHEST:
         cc = plane_peer(i)
         remote(val_send.at[cc], val_recv.at[i], s7.at[i], r7.at[i], cc, h, p).start()
-        return carry
+
+    def drain(src, dst, ss, rs):
+        def left(i, carry):
+            remote(src.at[c], dst.at[i], ss.at[i], rs.at[i], c, h, p).wait_send()
+            return carry
+
+        lax.fori_loop(1, PLANE, left, 0)
 
     for copy in loads[3:8] + loads[10:]:
         copy.wait()
@@ -196,9 +190,7 @@
             l_v[b * 2 + k] = jnp.broadcast_to(l[:, lanes], (8, CHUNK))
         return carry
 
-    lax.fori_loop(0, EARLY, cached_block, 0)
-    lax.fori_loop(1, PLANE, send_values, 0)
-    lax.fori_loop(EARLY, 8, cached_block, 0)
+    lax.fori_loop(0, 8, cached_block, 0)
 
     mine = jnp.dot(
         st_v[pl.ds(pl.multiple_of(c * NEW_CHIP, NEW_CHIP), NEW_CHIP), :], w_v[...],
@@ -212,6 +204,7 @@
     keyz_send[...] = lax.fori_loop(1, PLANE, sum_keys, mine[:, :HD])
     swap = remote(keyz_send, keyz_recv, s2, r2, c, h, 1 - p)
     swap.start()
+    drain(key_send, key_recv, s1, r1)
 
     def sum_values(i, acc):
         remote(val_send.at[c], val_recv.at[i], s7.at[i], r7.at[i], c, h, p).wait_recv()
@@ -257,13 +250,14 @@
     for dy in (2, 1, 3, 0):
         new_block(dy)
 
-        def send_att(dx, carry, dy=dy):
+        for dx in (2, 1, 3, 0):
             i = dy * NX + dx
-            cc = ((y + dy) % NX) * NX + (x + dx) % NX
-            remote(att_send.at[cc], att_recv.at[i], s3.at[i], r3.at[i], cc, h, p).start()
-            return carry
-
-        lax.fori_loop(1 if dy == 0 else 0, NX, send_att, 0)
+            if i > 0:
+                cc = plane_peer(i)
+                remote(att_send.at[cc], att_recv.at[i], s3.at[i], r3.at[i], cc, h, p).start()
+
+    drain(val_send, val_recv, s7, r7)
+    swap.wait_send()
 
     def merge(state, block):
         acc, m, l = state
@@ -282,68 +276,64 @@
     attz_send[HD:MSG] = stat_rows(state[1], state[2])
     swap_att = remote(attz_send, attz_recv, s4, r4, c, h, 1 - p)
     swap_att.start()
+    to = lax.broadcasted_iota(jnp.int32, (CHUNK, CHUNK), 0)
+    frm = lax.broadcasted_iota(jnp.int32, (CHUNK, CHUNK), 1)
+    perm = jnp.where(frm == (to % 16) * GROUP + to // 16, 1.0, 0.0).astype(BF16)
+    drain(att_send, att_recv, s3, r3)
     swap_att.wait_recv()
     acc, _, l = merge(state, attz_recv[...])
     att = (acc / l).astype(BF16)
-    to = lax.broadcasted_iota(jnp.int32, (CHUNK, CHUNK), 0)
-    frm = lax.broadcasted_iota(jnp.int32, (CHUNK, CHUNK), 1)
-    perm = jnp.where(frm == (to % 16) * GROUP + to // 16, 1.0, 0.0).astype(BF16)
     ag_v[c] = mm(perm, att, 1, 1).astype(BF16)
 
-    def send_ag(i, carry):
+    for i in FARTHEST:
         remote(ag_v.at[c], ag_v.at[c], s5.at[i], r5.at[i], plane_peer(i), h, p).start()
+    swap_values.wait_recv()
+    nv_ref[...] = (valz_kept[...] + valz_recv[...].astype(F32)).astype(BF16)
+    swap_values.wait_send()
+    swap_att.wait_send()
+    loads[9].wait()
+
+    for dy in (0, 1, 3, 2):
+        yy = (y + NX - dy) % NX
+        for dx in range(NX):
+            i = dy * NX + dx
+            if i > 0:
+                src = yy * NX + (x + NX - dx) % NX
+                remote(ag_v.at[c], ag_v.at[src], s5.at[i], r5.at[i], c, h, p).wait_recv()
+        rows = ag_v[pl.ds(yy * NX, NX)]
+        out = jnp.zeros((NX * 16, OUT_COLS), F32)
+        for g in range(0, GROUP, 2):
+            a = jnp.concatenate(
+                [rows[:, (g + k) * 16:(g + k + 1) * 16, :].reshape(NX * 16, HD) for k in range(2)], 1
+            )
+            out = out + jnp.dot(a, ow_v[g * HD:(g + 2) * HD, :], preferred_element_type=F32)
+        part_v[pl.ds(yy * 2, 2)] = out.reshape(2, 32, OUT_COLS)
+        out_send[pl.ds(yy * 2, 2)] = out.astype(BF16).reshape(2, 32, OUT_COLS)
+        for k in range(2):
+            hh = yy * 2 + k
+            j = (hh + HEADS - h) % HEADS
+
+            @pl.when(j != 0)
+            def _():
+                remote(out_send.at[hh], out_recv.at[j], s6.at[j], r6.at[j], c, hh, p).start()
+
+    def left_ag(i, carry):
+        remote(ag_v.at[c], ag_v.at[c], s5.at[i], r5.at[i], c, h, p).wait_send()
         return carry
 
-    lax.fori_loop(1, PLANE, send_ag, 0)
-    loads[9].wait()
-
-    def wait_ag(i, carry):
-        src = ((y + NX - i // NX) % NX) * NX + (x + NX - i % NX) % NX
-        remote(ag_v.at[c], ag_v.at[src], s5.at[i], r5.at[i], c, h, p).wait_recv()
-        return carry
-
-    lax.fori_loop(1, PLANE, wait_ag, 0)
-
-    out = jnp.zeros((256, OUT_COLS), F32)
-    for g in range(GROUP):
-        a = ag_v[:, g * 16:(g + 1) * 16, :].reshape(256, HD)
-        out = out + jnp.dot(a, ow_v[g * HD:(g + 1) * HD, :], preferred_element_type=F32)
-    part_v[...] = out.reshape(HEADS, 32, OUT_COLS)
-    out_send[...] = out.astype(BF16).reshape(HEADS, 32, OUT_COLS)
-
-    def send_out(j, carry):
-        hh = (h + j) % HEADS
-        remote(out_send.at[hh], out_recv.at[j], s6.at[j], r6.at[j], c, hh, p).start()
-        return carry
-
-    lax.fori_loop(1, HEADS, send_out, 0)
+    lax.fori_loop(1, PLANE, left_ag, 0)
 
     def sum_out(j, acc):
         remote(out_send.at[h], out_recv.at[j], s6.at[j], r6.at[j], c, h, p).wait_recv()
         return acc + out_recv[j].astype(F32)
 
-    swap_values.wait_recv()
-    nv_ref[...] = (valz_kept[...] + valz_recv[...].astype(F32)).astype(BF16)
-
     proj_ref[...] = lax.fori_loop(1, HEADS, sum_out, part_v[h]).astype(BF16)
 
-    def drain(i, carry):
-        remote(key_send.at[c], key_recv.at[i], s1.at[i], r1.at[i], c, h, p).wait_send()
-        remote(val_send.at[c], val_recv.at[i], s7.at[i], r7.at[i], c, h, p).wait_send()
-        remote(att_send.at[c], att_recv.at[i], s3.at[i], r3.at[i], c, h, p).wait_send()
-        remote(ag_v.at[c], ag_v.at[c], s5.at[i], r5.at[i], c, h, p).wait_send()
-        return carry
-
-    lax.fori_loop(1, PLANE, drain, 0)
-    swap.wait_send()
-    swap_values.wait_send()
-    swap_att.wait_send()
-
-    def drain_out(j, carry):
+    def left_out(j, carry):
         remote(out_send.at[h], out_recv.at[j], s6.at[j], r6.at[j], c, h, p).wait_send()
         return carry
 
-    lax.fori_loop(1, HEADS, drain_out, 0)
+    lax.fori_loop(1, HEADS, left_out, 0)
 
 
 def body(

time: 54.3 us -> 52.3 us (0.963)
  Pallas kernels: 50.4 us -> 48.4 us
    pallas_call x1, Pallas kernels: 50.4 us -> 48.4 us  [body(): pl.pallas_call(kernel, out_shape=(jax.ShapeDtypeStruct((32, OUT_COLS), BF...]
where the time goes in v4:
time: 52.3 us; the launch traced here: 52.2 us
  Pallas kernels  48.4 us (93%)
  local copies, waits for them, and re-layouts  2.48 us (5%)
  between operations  1.3 us (2%)
    pallas_call x1, Pallas kernels, body(): pl.pallas_call(kernel, out_shape=(jax.ShapeDtypeStruct((32, OUT_COLS), BF...  48.4 us
    unnamed x5, local copies, waits for them, and re-layouts  2.48 us

profile of v4, /device:TPU:1, one launch (start us, length us, event | category | flops | bytes accessed | tf_op | source)
XLA Modules:
  0.0 52.2 jit_solution(13523263567879869276)
XLA Ops:
  1.3 0.0 copy-start
  1.3 0.7 %copy-done = s32[256]{0:T(256)S(1)} copy-done((s32[256]{0:T(256)S(1)}, s32[256]{0:T(256)}, u32[]{:S(2)}) %copy-start) | copy-done | bytes 1048
  2.0 48.4 %shard_map.139 = (bf16[32,256]{1,0:T(8,128)(2,1)S(1)}, bf16[48,128]{1,0:T(8,128)(2,1)S(1)}, bf16[48,128]{1,0:T(8,128)(2,1)S(1)}) custom-call(bf16[2048,128]{1,0:T(8,128)(2,1)} %bitcast.11, bf16[256,128]{1,0:T(8,128)(2,1)} %bitcast.12, bf16[256,128]{1,0:T(8,128)(2,1)} %bitcast.13, bf16[1536,256]{1,0:T(8,128)(2,1)} %st_hbm.1, bf16[256,128]{1,0:T(8,128)(2,1)} %kw_hbm.1, ...), custom_call_target="tpu_custom_call" | custom-call | tf_op jit(solution)/shard_map/pallas_call | solution.py:347
  50.3 0.6 %copy.19 = bf16[32,256]{1,0:T(8,128)(2,1)} copy(bf16[32,256]{1,0:T(8,128)(2,1)S(1)} %get-tuple-element.12) | data formatting | bytes 32768
  51.0 0.6 %copy.20 = bf16[48,1,128]{2,0,1:T(8,128)(2,1)} copy(bf16[48,1,128]{2,0,1:T(8,128)(2,1)S(1)} %bitcast.9) | data formatting | bytes 24576
  51.6 0.6 %copy.21 = bf16[48,1,128]{2,0,1:T(8,128)(2,1)} copy(bf16[48,1,128]{2,0,1:T(8,128)(2,1)S(1)} %bitcast.8) | data formatting | bytes 24576
Async XLA Ops:
  1.3 0.7 %copy-start = (s32[256]{0:T(256)S(1)}, s32[256]{0:T(256)}, u32[]{:S(2)}) copy-start(s32[256]{0:T(256)} %param.21) | copy-start | bytes 3076

commit v5 on v4

--- a/solution.py
+++ b/solution.py
@@ -26,7 +26,8 @@
 CHUNK = 128
 CACHED = 256
 SUFFIX = 256
-MSG = HD + 16
+HALF = HD // 2
+FIRST = HALF + 16
 OUT_COLS = 256
 SCALE = HD**-0.5
 
@@ -80,13 +81,13 @@
 
 def kernel(
     q_hbm, pk_hbm, pv_hbm, st_hbm, kw_hbm, vw_hbm, sk_hbm, sv_hbm, len_hbm, asg_hbm, ow_hbm, rot_hbm,
-    proj_ref, nk_ref, nv_ref,
+    proj_ref, kv_ref,
     st_v, w_v, q_v, k_v, v_v, vt_v, ow_v, rot_v, len_v, asg_v,
     key_send, key_recv, val_send, val_recv, keyz_send, keyz_recv, valz_send, valz_recv, valz_kept,
     acc_v, m_v, l_v,
-    att_send, att_recv, attz_send, attz_recv,
+    low_send, low_recv, high_send, high_recv, lowz_send, lowz_recv, highz_send, highz_recv,
     ag_v, part_v, out_send, out_recv,
-    lsem, s1, r1, s2, r2, s3, r3, s4, r4, s5, r5, s6, r6, s7, r7, s8, r8,
+    lsem, wsem, s1, r1, s2, r2, s3, r3, s4, r4, s5, r5, s6, r6, s7, r7, s8, r8, s9, r9, s10, r10, s11, r11,
 ):
     c = lax.axis_index("ctx")
     h = lax.axis_index("head")
@@ -129,11 +130,19 @@
         pltpu.make_async_copy(pv_hbm, v_v.at[pl.ds(0, CACHED)], lsem.at[6]),
         pltpu.make_async_copy(sv_hbm, v_v.at[pl.ds(CACHED, SUFFIX)], lsem.at[7]),
         pltpu.make_async_copy(rot_hbm.at[c], rot_v, lsem.at[8]),
-        pltpu.make_async_copy(ow_hbm, ow_v, lsem.at[9]),
-        pltpu.make_async_copy(len_hbm, len_v, lsem.at[10]),
-        pltpu.make_async_copy(asg_hbm, asg_v, lsem.at[11]),
+        pltpu.make_async_copy(len_hbm, len_v, lsem.at[9]),
+        pltpu.make_async_copy(asg_hbm, asg_v, lsem.at[10]),
     ]
-    for copy in loads:
+    weights = [
+        pltpu.make_async_copy(
+            ow_hbm.at[pl.ds(g * HD + f * HALF, HALF)],
+            ow_v.at[f, pl.ds(g * HALF, HALF)],
+            wsem.at[f * GROUP + g],
+        )
+        for f in range(2)
+        for g in range(GROUP)
+    ]
+    for copy in loads + weights:
         copy.start()
 
     for copy in loads[:3]:
@@ -159,7 +168,7 @@
 
         lax.fori_loop(1, PLANE, left, 0)
 
-    for copy in loads[3:8] + loads[10:]:
+    for copy in loads[3:8] + loads[9:]:
         copy.wait()
     vt_v[...] = v_v[...].astype(F32).T.astype(BF16)
     suffix_id = shard
@@ -222,7 +231,7 @@
     raw = keyz_send[...] + keyz_recv[...]
     turned = pltpu.roll(raw, HD // 2, 1)
     new_k = (raw * rot_v[:, :HD] + turned * rot_v[:, HD:]).astype(BF16)
-    nk_ref[...] = jnp.where(first, new_k[:NEW_DEV], new_k[NEW_DEV:])
+    kv_ref[0] = jnp.where(first, new_k[:NEW_DEV], new_k[NEW_DEV:])
     token = lax.broadcasted_iota(jnp.int32, (NEW_CHIP, CHUNK), 0)
     counted = jnp.where((token // NEW_DEV) == p, 1.0, 0.0).astype(F32)
 
@@ -240,8 +249,9 @@
             e = jnp.exp(s[:, lanes] - m_new)
             l_new = l_v[cc][0:1] * shrink + jnp.sum(e * counted, 0, keepdims=True)
             o = acc_v[cc] * shrink + mm(new_vt, e.astype(BF16), 1, 0)
-            att_send[cc, 0:HD] = o.astype(BF16)
-            att_send[cc, HD:MSG] = stat_rows(m_new, l_new)
+            low_send[cc, 0:HALF] = o[:HALF].astype(BF16)
+            low_send[cc, HALF:FIRST] = stat_rows(m_new, l_new)
+            high_send[cc] = o[HALF:].astype(BF16)
             if dy == 0:
                 acc_v[cc] = o
                 m_v[cc] = jnp.broadcast_to(m_new, (8, CHUNK))
@@ -254,59 +264,92 @@
             i = dy * NX + dx
             if i > 0:
                 cc = plane_peer(i)
-                remote(att_send.at[cc], att_recv.at[i], s3.at[i], r3.at[i], cc, h, p).start()
+                remote(low_send.at[cc], low_recv.at[i], s3.at[i], r3.at[i], cc, h, p).start()
+    for i in FARTHEST:
+        cc = plane_peer(i)
+        remote(low_send.at[cc], low_recv.at[i], s3.at[i], r3.at[i], cc, h, p).wait_send()
+        remote(high_send.at[cc], high_recv.at[i], s9.at[i], r9.at[i], cc, h, p).start()
 
     drain(val_send, val_recv, s7, r7)
     swap.wait_send()
 
-    def merge(state, block):
+    def sum_low(i, state):
+        remote(low_send.at[c], low_recv.at[i], s3.at[i], r3.at[i], c, h, p).wait_recv()
         acc, m, l = state
-        m_in, l_in = read_stats(block[HD:MSG])
+        m_in, l_in = read_stats(low_recv[i, HALF:FIRST])
         m_all = jnp.maximum(m, m_in)
         a = jnp.exp(m - m_all)
         b = jnp.exp(m_in - m_all)
-        return (acc * a + block[0:HD].astype(F32) * b, m_all, l * a + l_in * b)
-
-    def sum_att(i, state):
-        remote(att_send.at[c], att_recv.at[i], s3.at[i], r3.at[i], c, h, p).wait_recv()
-        return merge(state, att_recv[i])
-
-    state = lax.fori_loop(1, PLANE, sum_att, (acc_v[c], m_v[c][0:1], l_v[c][0:1]))
-    attz_send[0:HD] = state[0].astype(BF16)
-    attz_send[HD:MSG] = stat_rows(state[1], state[2])
-    swap_att = remote(attz_send, attz_recv, s4, r4, c, h, 1 - p)
-    swap_att.start()
-    to = lax.broadcasted_iota(jnp.int32, (CHUNK, CHUNK), 0)
-    frm = lax.broadcasted_iota(jnp.int32, (CHUNK, CHUNK), 1)
-    perm = jnp.where(frm == (to % 16) * GROUP + to // 16, 1.0, 0.0).astype(BF16)
-    drain(att_send, att_recv, s3, r3)
-    swap_att.wait_recv()
-    acc, _, l = merge(state, attz_recv[...])
-    att = (acc / l).astype(BF16)
-    ag_v[c] = mm(perm, att, 1, 1).astype(BF16)
-
-    for i in FARTHEST:
-        remote(ag_v.at[c], ag_v.at[c], s5.at[i], r5.at[i], plane_peer(i), h, p).start()
+        return (acc * a + low_recv[i, 0:HALF].astype(F32) * b, m_all, l * a + l_in * b)
+
+    own_m = m_v[c][0:1]
+    low, m, l = lax.fori_loop(1, PLANE, sum_low, (acc_v[c, 0:HALF], own_m, l_v[c][0:1]))
+    lowz_send[0:HALF] = low.astype(BF16)
+    lowz_send[HALF:FIRST] = stat_rows(m, l)
+    swap_low = remote(lowz_send, lowz_recv, s4, r4, c, h, 1 - p)
+    swap_low.start()
+
+    def sum_high(i, acc):
+        remote(high_send.at[c], high_recv.at[i], s9.at[i], r9.at[i], c, h, p).wait_recv()
+        m_in, _ = read_stats(low_recv[i, HALF:FIRST])
+        return acc + high_recv[i].astype(F32) * jnp.exp(m_in - m)
+
+    high = lax.fori_loop(1, PLANE, sum_high, acc_v[c, HALF:HD] * jnp.exp(own_m - m))
+    highz_send[...] = high.astype(BF16)
+    swap_high = remote(highz_send, highz_recv, s10, r10, c, h, 1 - p)
+    swap_high.start()
+
+    to = lax.broadcasted_iota(jnp.int32, (HALF, CHUNK), 0)
+    frm = lax.broadcasted_iota(jnp.int32, (HALF, CHUNK), 1)
+    perms = [
+        jnp.where(frm == (to % 16) * GROUP + (to // 16) * 2 + k, 1.0, 0.0).astype(BF16)
+        for k in range(2)
+    ]
+    drain(high_send, high_recv, s9, r9)
+
+    swap_low.wait_recv()
+    m_in, l_in = read_stats(lowz_recv[HALF:FIRST])
+    m_all = jnp.maximum(m, m_in)
+    a = jnp.exp(m - m_all)
+    b = jnp.exp(m_in - m_all)
+    inverse = 1.0 / (l * a + l_in * b)
+    a, b = a * inverse, b * inverse
+
+    def share(f, mine, other, ss, rs):
+        att = (mine * a + other.astype(F32) * b).astype(BF16)
+        ag_v[f, c] = jnp.concatenate([mm(perm, att, 1, 1) for perm in perms], 1).astype(BF16)
+        for i in FARTHEST:
+            remote(ag_v.at[f, c], ag_v.at[f, c], ss.at[i], rs.at[i], plane_peer(i), h, p).start()
+
+    share(0, low, lowz_recv[0:HALF], s5, r5)
+    swap_high.wait_recv()
+    share(1, high, highz_recv[...], s11, r11)
     swap_values.wait_recv()
-    nv_ref[...] = (valz_kept[...] + valz_recv[...].astype(F32)).astype(BF16)
+    kv_ref[1] = (valz_kept[...] + valz_recv[...].astype(F32)).astype(BF16)
     swap_values.wait_send()
-    swap_att.wait_send()
-    loads[9].wait()
-
-    for dy in (0, 1, 3, 2):
-        yy = (y + NX - dy) % NX
+    swap_low.wait_send()
+    swap_high.wait_send()
+    for copy in weights:
+        copy.wait()
+
+    def product(f, yy, dy, ss, rs):
         for dx in range(NX):
             i = dy * NX + dx
             if i > 0:
                 src = yy * NX + (x + NX - dx) % NX
-                remote(ag_v.at[c], ag_v.at[src], s5.at[i], r5.at[i], c, h, p).wait_recv()
-        rows = ag_v[pl.ds(yy * NX, NX)]
-        out = jnp.zeros((NX * 16, OUT_COLS), F32)
-        for g in range(0, GROUP, 2):
-            a = jnp.concatenate(
-                [rows[:, (g + k) * 16:(g + k + 1) * 16, :].reshape(NX * 16, HD) for k in range(2)], 1
-            )
-            out = out + jnp.dot(a, ow_v[g * HD:(g + 2) * HD, :], preferred_element_type=F32)
+                remote(ag_v.at[f, c], ag_v.at[f, src], ss.at[i], rs.at[i], c, h, p).wait_recv()
+        rows = ag_v[f, pl.ds(yy * NX, NX)]
+        rows = jnp.concatenate(
+            [rows[:, k * 16:(k + 1) * 16, :].reshape(NX * 16, HD) for k in range(GROUP // 2)], 1
+        )
+        return jnp.dot(rows, ow_v[f], preferred_element_type=F32)
+
+    for dy in (0, 1, 3, 2):
+        yy = (y + NX - dy) % NX
+        part_v[pl.ds(yy * 2, 2)] = product(0, yy, dy, s5, r5).reshape(2, 32, OUT_COLS)
+    for dy in (0, 1, 3, 2):
+        yy = (y + NX - dy) % NX
+        out = part_v[pl.ds(yy * 2, 2)].reshape(NX * 16, OUT_COLS) + product(1, yy, dy, s11, r11)
         part_v[pl.ds(yy * 2, 2)] = out.reshape(2, 32, OUT_COLS)
         out_send[pl.ds(yy * 2, 2)] = out.astype(BF16).reshape(2, 32, OUT_COLS)
         for k in range(2):
@@ -318,7 +361,8 @@
                 remote(out_send.at[hh], out_recv.at[j], s6.at[j], r6.at[j], c, hh, p).start()
 
     def left_ag(i, carry):
-        remote(ag_v.at[c], ag_v.at[c], s5.at[i], r5.at[i], c, h, p).wait_send()
+        remote(ag_v.at[0, c], ag_v.at[0, c], s5.at[i], r5.at[i], c, h, p).wait_send()
+        remote(ag_v.at[1, c], ag_v.at[1, c], s11.at[i], r11.at[i], c, h, p).wait_send()
         return carry
 
     lax.fori_loop(1, PLANE, left_ag, 0)
@@ -344,15 +388,14 @@
     hbm = pl.BlockSpec(memory_space=pl.ANY)
     vmem = pl.BlockSpec(memory_space=pltpu.VMEM)
     dma = pltpu.SemaphoreType.DMA
-    projected, new_keys, new_values = pl.pallas_call(
+    projected, new_both = pl.pallas_call(
         kernel,
         out_shape=(
             jax.ShapeDtypeStruct((32, OUT_COLS), BF16),
-            jax.ShapeDtypeStruct((NEW_DEV, HD), BF16),
-            jax.ShapeDtypeStruct((NEW_DEV, HD), BF16),
+            jax.ShapeDtypeStruct((2, NEW_DEV, HD), BF16),
         ),
         in_specs=[hbm] * 12,
-        out_specs=(vmem, vmem, vmem),
+        out_specs=(vmem, vmem),
         scratch_shapes=[
             pltpu.VMEM((NEW, FEAT), BF16),
             pltpu.VMEM((FEAT, 2 * HD), BF16),
@@ -360,7 +403,7 @@
             pltpu.VMEM((CACHED + SUFFIX, HD), BF16),
             pltpu.VMEM((CACHED + SUFFIX, HD), BF16),
             pltpu.VMEM((HD, CACHED + SUFFIX), BF16),
-            pltpu.VMEM((GROUP * HD, OUT_COLS), BF16),
+            pltpu.VMEM((2, GROUP * HALF, OUT_COLS), BF16),
             pltpu.VMEM((NEW_CHIP, 2 * HD), F32),
             pltpu.SMEM((1,), jnp.int32),
             pltpu.VMEM((1, 256), jnp.int32),
@@ -376,15 +419,20 @@
             pltpu.VMEM((PLANE, HD, CHUNK), F32),
             pltpu.VMEM((PLANE, 8, CHUNK), F32),
             pltpu.VMEM((PLANE, 8, CHUNK), F32),
-            pltpu.VMEM((PLANE, MSG, CHUNK), BF16),
-            pltpu.VMEM((PLANE, MSG, CHUNK), BF16),
-            pltpu.VMEM((MSG, CHUNK), BF16),
-            pltpu.VMEM((MSG, CHUNK), BF16),
-            pltpu.VMEM((PLANE, CHUNK, HD), BF16),
+            pltpu.VMEM((PLANE, FIRST, CHUNK), BF16),
+            pltpu.VMEM((PLANE, FIRST, CHUNK), BF16),
+            pltpu.VMEM((PLANE, HALF, CHUNK), BF16),
+            pltpu.VMEM((PLANE, HALF, CHUNK), BF16),
+            pltpu.VMEM((FIRST, CHUNK), BF16),
+            pltpu.VMEM((FIRST, CHUNK), BF16),
+            pltpu.VMEM((HALF, CHUNK), BF16),
+            pltpu.VMEM((HALF, CHUNK), BF16),
+            pltpu.VMEM((2, PLANE, HALF, HD), BF16),
             pltpu.VMEM((HEADS, 32, OUT_COLS), F32),
             pltpu.VMEM((HEADS, 32, OUT_COLS), BF16),
             pltpu.VMEM((HEADS, 32, OUT_COLS), BF16),
-            dma((12,)),
+            dma((11,)),
+            dma((2 * GROUP,)),
             dma((PLANE,)), dma((PLANE,)),
             dma, dma,
             dma((PLANE,)), dma((PLANE,)),
@@ -393,6 +441,9 @@
             dma((HEADS,)), dma((HEADS,)),
             dma((PLANE,)), dma((PLANE,)),
             dma, dma,
+            dma((PLANE,)), dma((PLANE,)),
+            dma, dma,
+            dma((PLANE,)), dma((PLANE,)),
         ],
         compiler_params=pltpu.CompilerParams(
             collective_id=0, has_side_effects=True, vmem_limit_bytes=55168 * 1024
@@ -413,8 +464,8 @@
     )
     return (
         projected,
-        new_keys.reshape(NEW_DEV, 1, HD),
-        new_values.reshape(NEW_DEV, 1, HD),
+        new_both[0].reshape(NEW_DEV, 1, HD),
+        new_both[1].reshape(NEW_DEV, 1, HD),
     )
 
 

time: 52.3 us -> 51.2 us (0.979)
  local copies, waits for them, and re-layouts: 2.48 us -> 1.88 us
    unnamed x5 -> x3, local copies, waits for them, and re-layouts: 2.48 us -> 1.28 us
    another operation x0 -> x1, local copies, waits for them, and re-layouts: none -> 0.61 us  [body(): new_both[1].reshape(NEW_DEV, 1, HD)]
    pallas_call x1, Pallas kernels: 48.4 us -> 47.9 us  [body(): pl.pallas_call(kernel, out_shape=(jax.ShapeDtypeStruct((32, OUT_COLS), BF...]
where the time goes in v5:
time: 51.2 us; the launch traced here: 51 us
  Pallas kernels  47.9 us (94%)
  local copies, waits for them, and re-layouts  1.88 us (4%)
  between operations  1.3 us (3%)
    pallas_call x1, Pallas kernels, body(): pl.pallas_call(kernel, out_shape=(jax.ShapeDtypeStruct((32, OUT_COLS), BF...  47.9 us
    unnamed x3, local copies, waits for them, and re-layouts  1.28 us

profile of v5, /device:TPU:1, one launch (start us, length us, event | category | flops | bytes accessed | tf_op | source)
XLA Modules:
  0.0 51.0 jit_solution(10551183682041507624)
XLA Ops:
  1.3 0.0 copy-start
  1.3 0.7 %copy-done = s32[256]{0:T(256)S(1)} copy-done((s32[256]{0:T(256)S(1)}, s32[256]{0:T(256)}, u32[]{:S(2)}) %copy-start) | copy-done | bytes 1048
  2.0 47.9 %shard_map.139 = (bf16[32,256]{1,0:T(8,128)(2,1)S(1)}, bf16[2,48,128]{2,1,0:T(8,128)(2,1)S(1)}) custom-call(bf16[2048,128]{1,0:T(8,128)(2,1)} %bitcast.11, bf16[256,128]{1,0:T(8,128)(2,1)} %bitcast.12, bf16[256,128]{1,0:T(8,128)(2,1)} %bitcast.13, bf16[1536,256]{1,0:T(8,128)(2,1)} %st_hbm.1, bf16[256,128]{1,0:T(8,128)(2,1)} %kw_hbm.1, ...), custom_call_target="tpu_custom_call" | custom-call | tf_op jit(solution)/shard_map/pallas_call | solution.py:391
  49.8 0.6 %slice_bitcast_fusion = (bf16[48,1,128]{2,0,1:T(8,128)(2,1)}, bf16[48,1,128]{2,0,1:T(8,128)(2,1)}) fusion(bf16[2,48,128]{2,1,0:T(8,128)(2,1)S(1)} %get-tuple-element.6), kind=kLoop, calls=%fused_computation | loop fusion | bytes 49152 | tf_op jit(solution)/shard_map/reshape;squeeze | solution.py:468
  50.4 0.6 %copy.17 = bf16[32,256]{1,0:T(8,128)(2,1)} copy(bf16[32,256]{1,0:T(8,128)(2,1)S(1)} %get-tuple-element.12) | data formatting | bytes 32768
Async XLA Ops:
  1.3 0.7 %copy-start = (s32[256]{0:T(256)S(1)}, s32[256]{0:T(256)}, u32[]{:S(2)}) copy-start(s32[256]{0:T(256)} %param.21) | copy-start | bytes 3076

commit v6 on v5

--- a/solution.py
+++ b/solution.py
@@ -29,7 +29,7 @@
 HALF = HD // 2
 FIRST = HALF + 16
 OUT_COLS = 256
-SCALE = HD**-0.5
+SCALE = HD**-0.5 * math.log2(math.e)
 
 
 def hops(i):
@@ -105,20 +105,6 @@
             device_id_type=pl.DeviceIdType.MESH,
         )
 
-    barrier = pltpu.get_barrier_semaphore()
-
-    def greet(cc, hh, pp):
-        pl.semaphore_signal(
-            barrier, inc=1, device_id={"ctx": cc, "head": hh, "pool": pp},
-            device_id_type=pl.DeviceIdType.MESH,
-        )
-
-    for i in FARTHEST:
-        greet(plane_peer(i), h, p)
-    greet(c, h, 1 - p)
-    for j in range(1, HEADS):
-        greet(c, (h + j) % HEADS, p)
-
     shard = c * POOL + p
     loads = [
         pltpu.make_async_copy(st_hbm, st_v, lsem.at[0]),
@@ -134,16 +120,24 @@
         pltpu.make_async_copy(asg_hbm, asg_v, lsem.at[10]),
     ]
     weights = [
-        pltpu.make_async_copy(
-            ow_hbm.at[pl.ds(g * HD + f * HALF, HALF)],
-            ow_v.at[f, pl.ds(g * HALF, HALF)],
-            wsem.at[f * GROUP + g],
+        pltpu.make_async_copy(ow_hbm.at[:, f], ow_v.at[f], wsem.at[f]) for f in range(2)
+    ]
+    for copy in loads[:3]:
+        copy.start()
+
+    barrier = pltpu.get_barrier_semaphore()
+
+    def greet(cc, hh, pp):
+        pl.semaphore_signal(
+            barrier, inc=1, device_id={"ctx": cc, "head": hh, "pool": pp},
+            device_id_type=pl.DeviceIdType.MESH,
         )
-        for f in range(2)
-        for g in range(GROUP)
-    ]
-    for copy in loads + weights:
-        copy.start()
+
+    for i in FARTHEST:
+        greet(plane_peer(i), h, p)
+    greet(c, h, 1 - p)
+    for j in range(1, HEADS):
+        greet(c, (h + j) % HEADS, p)
 
     for copy in loads[:3]:
         copy.wait()
@@ -157,9 +151,11 @@
     for i in FARTHEST:
         cc = plane_peer(i)
         remote(key_send.at[cc], key_recv.at[i], s1.at[i], r1.at[i], cc, h, p).start()
-    for i in FARTHEST:
-        cc = plane_peer(i)
-        remote(val_send.at[cc], val_recv.at[i], s7.at[i], r7.at[i], cc, h, p).start()
+    for copy in loads[3:]:
+        copy.start()
+
+    for copy in weights:
+        copy.start()
 
     def drain(src, dst, ss, rs):
         def left(i, carry):
@@ -187,8 +183,8 @@
         m = jnp.maximum(
             jnp.max(s[:CACHED], 0, keepdims=True), jnp.max(side, 0, keepdims=True)
         )
-        main_e = jnp.exp(s[:CACHED] - m)
-        side_e = jnp.exp(side - m)
+        main_e = jnp.exp2(s[:CACHED] - m)
+        side_e = jnp.exp2(side - m)
         l = jnp.sum(main_e, 0, keepdims=True) + jnp.sum(side_e, 0, keepdims=True)
         e = jnp.concatenate([main_e.astype(BF16), side_e.astype(BF16)], 0)
         o = mm(vt_v[...], e, 1, 0)
@@ -199,7 +195,11 @@
             l_v[b * 2 + k] = jnp.broadcast_to(l[:, lanes], (8, CHUNK))
         return carry
 
-    lax.fori_loop(0, 8, cached_block, 0)
+    lax.fori_loop(0, 6, cached_block, 0, unroll=2)
+    for i in FARTHEST:
+        cc = plane_peer(i)
+        remote(val_send.at[cc], val_recv.at[i], s7.at[i], r7.at[i], cc, h, p).start()
+    lax.fori_loop(6, 8, cached_block, 0, unroll=2)
 
     mine = jnp.dot(
         st_v[pl.ds(pl.multiple_of(c * NEW_CHIP, NEW_CHIP), NEW_CHIP), :], w_v[...],
@@ -245,8 +245,8 @@
             cc = yy * NX + k
             m_old = m_v[cc][0:1]
             m_new = jnp.maximum(m_old, s_max[:, lanes])
-            shrink = jnp.exp(m_old - m_new)
-            e = jnp.exp(s[:, lanes] - m_new)
+            shrink = jnp.exp2(m_old - m_new)
+            e = jnp.exp2(s[:, lanes] - m_new)
             l_new = l_v[cc][0:1] * shrink + jnp.sum(e * counted, 0, keepdims=True)
             o = acc_v[cc] * shrink + mm(new_vt, e.astype(BF16), 1, 0)
             low_send[cc, 0:HALF] = o[:HALF].astype(BF16)
@@ -278,8 +278,8 @@
         acc, m, l = state
         m_in, l_in = read_stats(low_recv[i, HALF:FIRST])
         m_all = jnp.maximum(m, m_in)
-        a = jnp.exp(m - m_all)
-        b = jnp.exp(m_in - m_all)
+        a = jnp.exp2(m - m_all)
+        b = jnp.exp2(m_in - m_all)
         return (acc * a + low_recv[i, 0:HALF].astype(F32) * b, m_all, l * a + l_in * b)
 
     own_m = m_v[c][0:1]
@@ -292,9 +292,9 @@
     def sum_high(i, acc):
         remote(high_send.at[c], high_recv.at[i], s9.at[i], r9.at[i], c, h, p).wait_recv()
         m_in, _ = read_stats(low_recv[i, HALF:FIRST])
-        return acc + high_recv[i].astype(F32) * jnp.exp(m_in - m)
-
-    high = lax.fori_loop(1, PLANE, sum_high, acc_v[c, HALF:HD] * jnp.exp(own_m - m))
+        return acc + high_recv[i].astype(F32) * jnp.exp2(m_in - m)
+
+    high = lax.fori_loop(1, PLANE, sum_high, acc_v[c, HALF:HD] * jnp.exp2(own_m - m))
     highz_send[...] = high.astype(BF16)
     swap_high = remote(highz_send, highz_recv, s10, r10, c, h, 1 - p)
     swap_high.start()
@@ -310,8 +310,8 @@
     swap_low.wait_recv()
     m_in, l_in = read_stats(lowz_recv[HALF:FIRST])
     m_all = jnp.maximum(m, m_in)
-    a = jnp.exp(m - m_all)
-    b = jnp.exp(m_in - m_all)
+    a = jnp.exp2(m - m_all)
+    b = jnp.exp2(m_in - m_all)
     inverse = 1.0 / (l * a + l_in * b)
     a, b = a * inverse, b * inverse
 
@@ -342,7 +342,7 @@
         rows = jnp.concatenate(
             [rows[:, k * 16:(k + 1) * 16, :].reshape(NX * 16, HD) for k in range(GROUP // 2)], 1
         )
-        return jnp.dot(rows, ow_v[f], preferred_element_type=F32)
+        return jnp.dot(rows, ow_v[f].reshape(GROUP * HALF, OUT_COLS), preferred_element_type=F32)
 
     for dy in (0, 1, 3, 2):
         yy = (y + NX - dy) % NX
@@ -403,7 +403,7 @@
             pltpu.VMEM((CACHED + SUFFIX, HD), BF16),
             pltpu.VMEM((CACHED + SUFFIX, HD), BF16),
             pltpu.VMEM((HD, CACHED + SUFFIX), BF16),
-            pltpu.VMEM((2, GROUP * HALF, OUT_COLS), BF16),
+            pltpu.VMEM((2, GROUP, HALF, OUT_COLS), BF16),
             pltpu.VMEM((NEW_CHIP, 2 * HD), F32),
             pltpu.SMEM((1,), jnp.int32),
             pltpu.VMEM((1, 256), jnp.int32),
@@ -432,7 +432,7 @@
             pltpu.VMEM((HEADS, 32, OUT_COLS), BF16),
             pltpu.VMEM((HEADS, 32, OUT_COLS), BF16),
             dma((11,)),
-            dma((2 * GROUP,)),
+            dma((2,)),
             dma((PLANE,)), dma((PLANE,)),
             dma, dma,
             dma((PLANE,)), dma((PLANE,)),
@@ -459,7 +459,7 @@
         suffix_values.reshape(SUFFIX, HD),
         suffix_lengths,
         assignment.reshape(1, 256),
-        out_weight,
+        out_weight.reshape(GROUP, 2, HALF, OUT_COLS),
         rot,
     )
     return (

time: 51.2 us -> 50.1 us (0.979)
  Pallas kernels: 47.9 us -> 46.8 us
    pallas_call x1, Pallas kernels: 47.9 us -> 46.8 us  [body(): pl.pallas_call(kernel, out_shape=(jax.ShapeDtypeStruct((32, OUT_COLS), BF...]
where the time goes in v6:
time: 50.1 us; the launch traced here: 49.9 us
  Pallas kernels  46.8 us (93%)
  local copies, waits for them, and re-layouts  1.88 us (4%)
  between operations  1.3 us (3%)
    pallas_call x1, Pallas kernels, body(): pl.pallas_call(kernel, out_shape=(jax.ShapeDtypeStruct((32, OUT_COLS), BF...  46.8 us
    unnamed x3, local copies, waits for them, and re-layouts  1.28 us

profile of v6, /device:TPU:1, one launch (start us, length us, event | category | flops | bytes accessed | tf_op | source)
XLA Modules:
  0.0 49.9 jit_solution(4961830164319424531)
XLA Ops:
  1.3 0.0 copy-start
  1.3 0.7 %copy-done = s32[256]{0:T(256)S(1)} copy-done((s32[256]{0:T(256)S(1)}, s32[256]{0:T(256)}, u32[]{:S(2)}) %copy-start) | copy-done | bytes 1048
  2.0 46.8 %shard_map.139 = (bf16[32,256]{1,0:T(8,128)(2,1)S(1)}, bf16[2,48,128]{2,1,0:T(8,128)(2,1)S(1)}) custom-call(bf16[2048,128]{1,0:T(8,128)(2,1)} %bitcast.12, bf16[256,128]{1,0:T(8,128)(2,1)} %bitcast.14, bf16[256,128]{1,0:T(8,128)(2,1)} %bitcast.15, bf16[1536,256]{1,0:T(8,128)(2,1)} %st_hbm.1, bf16[256,128]{1,0:T(8,128)(2,1)} %kw_hbm.1, ...), custom_call_target="tpu_custom_call" | custom-call | tf_op jit(solution)/shard_map/pallas_call | solution.py:391
  48.7 0.6 %slice_bitcast_fusion = (bf16[48,1,128]{2,0,1:T(8,128)(2,1)}, bf16[48,1,128]{2,0,1:T(8,128)(2,1)}) fusion(bf16[2,48,128]{2,1,0:T(8,128)(2,1)S(1)} %get-tuple-element.6), kind=kLoop, calls=%fused_computation | loop fusion | bytes 49152 | tf_op jit(solution)/shard_map/reshape;squeeze | solution.py:468
  49.3 0.6 %copy.17 = bf16[32,256]{1,0:T(8,128)(2,1)} copy(bf16[32,256]{1,0:T(8,128)(2,1)S(1)} %get-tuple-element.12) | data formatting | bytes 32768
Async XLA Ops:
  1.3 0.7 %copy-start = (s32[256]{0:T(256)S(1)}, s32[256]{0:T(256)}, u32[]{:S(2)}) copy-start(s32[256]{0:T(256)} %param.21) | copy-start | bytes 3076

commit v7 on v6

--- a/solution.py
+++ b/solution.py
@@ -195,7 +195,7 @@
             l_v[b * 2 + k] = jnp.broadcast_to(l[:, lanes], (8, CHUNK))
         return carry
 
-    lax.fori_loop(0, 6, cached_block, 0, unroll=2)
+    lax.fori_loop(0, 6, cached_block, 0, unroll=3)
     for i in FARTHEST:
         cc = plane_peer(i)
         remote(val_send.at[cc], val_recv.at[i], s7.at[i], r7.at[i], cc, h, p).start()
@@ -273,17 +273,24 @@
     drain(val_send, val_recv, s7, r7)
     swap.wait_send()
 
+    own_m = m_v[c][0:1]
+
+
+    def largest(i, m):
+        remote(low_send.at[c], low_recv.at[i], s3.at[i], r3.at[i], c, h, p).wait_recv()
+        return jnp.maximum(m, read_stats(low_recv[i, HALF:FIRST])[0])
+
+    m = lax.fori_loop(1, PLANE, largest, own_m)
+
     def sum_low(i, state):
-        remote(low_send.at[c], low_recv.at[i], s3.at[i], r3.at[i], c, h, p).wait_recv()
-        acc, m, l = state
         m_in, l_in = read_stats(low_recv[i, HALF:FIRST])
-        m_all = jnp.maximum(m, m_in)
-        a = jnp.exp2(m - m_all)
-        b = jnp.exp2(m_in - m_all)
-        return (acc * a + low_recv[i, 0:HALF].astype(F32) * b, m_all, l * a + l_in * b)
-
-    own_m = m_v[c][0:1]
-    low, m, l = lax.fori_loop(1, PLANE, sum_low, (acc_v[c, 0:HALF], own_m, l_v[c][0:1]))
+        b = jnp.exp2(m_in - m)
+        return (state[0] + low_recv[i, 0:HALF].astype(F32) * b, state[1] + l_in * b)
+
+    a = jnp.exp2(own_m - m)
+    low, l = lax.fori_loop(
+        1, PLANE, sum_low, (acc_v[c, 0:HALF] * a, l_v[c][0:1] * a), unroll=5
+    )
     lowz_send[0:HALF] = low.astype(BF16)
     lowz_send[HALF:FIRST] = stat_rows(m, l)
     swap_low = remote(lowz_send, lowz_recv, s4, r4, c, h, 1 - p)
@@ -294,7 +301,7 @@
         m_in, _ = read_stats(low_recv[i, HALF:FIRST])
         return acc + high_recv[i].astype(F32) * jnp.exp2(m_in - m)
 
-    high = lax.fori_loop(1, PLANE, sum_high, acc_v[c, HALF:HD] * jnp.exp2(own_m - m))
+    high = lax.fori_loop(1, PLANE, sum_high, acc_v[c, HALF:HD] * jnp.exp2(own_m - m), unroll=5)
     highz_send[...] = high.astype(BF16)
     swap_high = remote(highz_send, highz_recv, s10, r10, c, h, 1 - p)
     swap_high.start()
@@ -371,7 +378,7 @@
         remote(out_send.at[h], out_recv.at[j], s6.at[j], r6.at[j], c, h, p).wait_recv()
         return acc + out_recv[j].astype(F32)
 
-    proj_ref[...] = lax.fori_loop(1, HEADS, sum_out, part_v[h]).astype(BF16)
+    proj_ref[...] = lax.fori_loop(1, HEADS, sum_out, part_v[h], unroll=True).astype(BF16)
 
     def left_out(j, carry):
         remote(out_send.at[h], out_recv.at[j], s6.at[j], r6.at[j], c, h, p).wait_send()

time: 50.1 us -> 50 us (level)
  no operation moved by 1% of the time
where the time goes in v7:
time: 50 us; the launch traced here: 49.8 us
  Pallas kernels  46.7 us (93%)
  local copies, waits for them, and re-layouts  1.88 us (4%)
  between operations  1.3 us (3%)
    pallas_call x1, Pallas kernels, body(): pl.pallas_call(kernel, out_shape=(jax.ShapeDtypeStruct((32, OUT_COLS), BF...  46.7 us
    unnamed x3, local copies, waits for them, and re-layouts  1.28 us

profile of v7, /device:TPU:1, one launch (start us, length us, event | category | flops | bytes accessed | tf_op | source)
XLA Modules:
  0.0 49.8 jit_solution(16307839366670376448)
XLA Ops:
  1.3 0.0 copy-start
  1.3 0.7 %copy-done = s32[256]{0:T(256)S(1)} copy-done((s32[256]{0:T(256)S(1)}, s32[256]{0:T(256)}, u32[]{:S(2)}) %copy-start) | copy-done | bytes 1048
  2.0 46.7 %shard_map.139 = (bf16[32,256]{1,0:T(8,128)(2,1)S(1)}, bf16[2,48,128]{2,1,0:T(8,128)(2,1)S(1)}) custom-call(bf16[2048,128]{1,0:T(8,128)(2,1)} %bitcast.12, bf16[256,128]{1,0:T(8,128)(2,1)} %bitcast.14, bf16[256,128]{1,0:T(8,128)(2,1)} %bitcast.15, bf16[1536,256]{1,0:T(8,128)(2,1)} %st_hbm.1, bf16[256,128]{1,0:T(8,128)(2,1)} %kw_hbm.1, ...), custom_call_target="tpu_custom_call" | custom-call | tf_op jit(solution)/shard_map/pallas_call | solution.py:398
  48.6 0.6 %slice_bitcast_fusion = (bf16[48,1,128]{2,0,1:T(8,128)(2,1)}, bf16[48,1,128]{2,0,1:T(8,128)(2,1)}) fusion(bf16[2,48,128]{2,1,0:T(8,128)(2,1)S(1)} %get-tuple-element.6), kind=kLoop, calls=%fused_computation | loop fusion | bytes 49152 | tf_op jit(solution)/shard_map/reshape;squeeze | solution.py:475
  49.2 0.6 %copy.17 = bf16[32,256]{1,0:T(8,128)(2,1)} copy(bf16[32,256]{1,0:T(8,128)(2,1)S(1)} %get-tuple-element.12) | data formatting | bytes 32768
Async XLA Ops:
  1.3 0.7 %copy-start = (s32[256]{0:T(256)S(1)}, s32[256]{0:T(256)}, u32[]{:S(2)}) copy-start(s32[256]{0:T(256)} %param.21) | copy-start | bytes 3076

commit v8 on v6

--- a/solution.py
+++ b/solution.py
@@ -195,7 +195,7 @@
             l_v[b * 2 + k] = jnp.broadcast_to(l[:, lanes], (8, CHUNK))
         return carry
 
-    lax.fori_loop(0, 6, cached_block, 0, unroll=2)
+    lax.fori_loop(0, 6, cached_block, 0, unroll=3)
     for i in FARTHEST:
         cc = plane_peer(i)
         remote(val_send.at[cc], val_recv.at[i], s7.at[i], r7.at[i], cc, h, p).start()
@@ -221,17 +221,12 @@
 
     values = lax.fori_loop(1, PLANE, sum_values, mine[:, HD:])
     first = p == 0
-    valz_send[...] = jnp.where(first, values[NEW_DEV:], values[:NEW_DEV]).astype(BF16)
-    valz_kept[...] = jnp.where(first, values[:NEW_DEV], values[NEW_DEV:])
-    swap_values = remote(valz_send, valz_recv, s8, r8, c, h, 1 - p)
-    swap_values.start()
     new_vt = values.T.astype(BF16)
     loads[8].wait()
     swap.wait_recv()
     raw = keyz_send[...] + keyz_recv[...]
     turned = pltpu.roll(raw, HD // 2, 1)
     new_k = (raw * rot_v[:, :HD] + turned * rot_v[:, HD:]).astype(BF16)
-    kv_ref[0] = jnp.where(first, new_k[:NEW_DEV], new_k[NEW_DEV:])
     token = lax.broadcasted_iota(jnp.int32, (NEW_CHIP, CHUNK), 0)
     counted = jnp.where((token // NEW_DEV) == p, 1.0, 0.0).astype(F32)
 
@@ -270,6 +265,11 @@
         remote(low_send.at[cc], low_recv.at[i], s3.at[i], r3.at[i], cc, h, p).wait_send()
         remote(high_send.at[cc], high_recv.at[i], s9.at[i], r9.at[i], cc, h, p).start()
 
+    kv_ref[0] = jnp.where(first, new_k[:NEW_DEV], new_k[NEW_DEV:])
+    valz_send[...] = jnp.where(first, values[NEW_DEV:], values[:NEW_DEV]).astype(BF16)
+    valz_kept[...] = jnp.where(first, values[:NEW_DEV], values[NEW_DEV:])
+    swap_values = remote(valz_send, valz_recv, s8, r8, c, h, 1 - p)
+    swap_values.start()
     drain(val_send, val_recv, s7, r7)
     swap.wait_send()
 
@@ -371,7 +371,7 @@
         remote(out_send.at[h], out_recv.at[j], s6.at[j], r6.at[j], c, h, p).wait_recv()
         return acc + out_recv[j].astype(F32)
 
-    proj_ref[...] = lax.fori_loop(1, HEADS, sum_out, part_v[h]).astype(BF16)
+    proj_ref[...] = lax.fori_loop(1, HEADS, sum_out, part_v[h], unroll=True).astype(BF16)
 
     def left_out(j, carry):
         remote(out_send.at[h], out_recv.at[j], s6.at[j], r6.at[j], c, h, p).wait_send()

time: 50.1 us -> 50 us (level)
  no operation moved by 1% of the time
where the time goes in v8:
time: 50 us; the launch traced here: 49.9 us
  Pallas kernels  46.7 us (93%)
  local copies, waits for them, and re-layouts  1.88 us (4%)
  between operations  1.3 us (3%)
    pallas_call x1, Pallas kernels, body(): pl.pallas_call(kernel, out_shape=(jax.ShapeDtypeStruct((32, OUT_COLS), BF...  46.7 us
    unnamed x3, local copies, waits for them, and re-layouts  1.28 us

profile of v8, /device:TPU:1, one launch (start us, length us, event | category | flops | bytes accessed | tf_op | source)
XLA Modules:
  0.0 49.9 jit_solution(17287284164886888387)
XLA Ops:
  1.3 0.0 copy-start
  1.3 0.7 %copy-done = s32[256]{0:T(256)S(1)} copy-done((s32[256]{0:T(256)S(1)}, s32[256]{0:T(256)}, u32[]{:S(2)}) %copy-start) | copy-done | bytes 1048
  2.0 46.7 %shard_map.139 = (bf16[32,256]{1,0:T(8,128)(2,1)S(1)}, bf16[2,48,128]{2,1,0:T(8,128)(2,1)S(1)}) custom-call(bf16[2048,128]{1,0:T(8,128)(2,1)} %bitcast.12, bf16[256,128]{1,0:T(8,128)(2,1)} %bitcast.14, bf16[256,128]{1,0:T(8,128)(2,1)} %bitcast.15, bf16[1536,256]{1,0:T(8,128)(2,1)} %st_hbm.1, bf16[256,128]{1,0:T(8,128)(2,1)} %kw_hbm.1, ...), custom_call_target="tpu_custom_call" | custom-call | tf_op jit(solution)/shard_map/pallas_call | solution.py:391
  48.7 0.6 %slice_bitcast_fusion = (bf16[48,1,128]{2,0,1:T(8,128)(2,1)}, bf16[48,1,128]{2,0,1:T(8,128)(2,1)}) fusion(bf16[2,48,128]{2,1,0:T(8,128)(2,1)S(1)} %get-tuple-element.6), kind=kLoop, calls=%fused_computation | loop fusion | bytes 49152 | tf_op jit(solution)/shard_map/reshape;squeeze | solution.py:468
  49.3 0.6 %copy.17 = bf16[32,256]{1,0:T(8,128)(2,1)} copy(bf16[32,256]{1,0:T(8,128)(2,1)S(1)} %get-tuple-element.12) | data formatting | bytes 32768
Async XLA Ops:
  1.3 0.7 %copy-start = (s32[256]{0:T(256)S(1)}, s32[256]{0:T(256)}, u32[]{:S(2)}) copy-start(s32[256]{0:T(256)} %param.21) | copy-start | bytes 3076
